TPU v7x, 32 devices: a whole 2x2x4 slice. The times are simulated.
32 devices in a mesh: section: 2 (over x), dp: 16 (over z, y, core).
Axes of the slice: x: 2, y: 2, z: 4, core: 2. Of those that a mesh axis runs over, the one named last changes fastest.
Arguments:
- text_in: bfloat16 [10240, 768], P('dp'), may hold values from -6 to 6
- cotangent: bfloat16 [10240, 768], P('dp'), may hold values from -6 to 6
- images: bfloat16 [256, 145, 1024], P('dp'), may hold values from -6 to 6
- segment_ids: int32 [256, 40], P('dp'), may hold values from 0 to 2, never falling along the last dimension, each value on 1 to 24 neighbouring positions
- row_image: int32 [64, 4], P('dp'), may hold values from 0 to 3, each once within a row
- self_qkv: bfloat16 [2, 768, 2304], P('section'), may hold values from -0.21875 to 0.21875
- self_out: bfloat16 [2, 768, 768], P('section'), may hold values from -0.75 to 0.75
- ffn_up: bfloat16 [2, 768, 3072], P('section'), may hold values from -0.21875 to 0.21875
- ffn_down: bfloat16 [2, 3072, 768], P('section'), may hold values from -0.109375 to 0.109375
- norm_gain: float32 [2, 2, 768], P('section'), may hold values from 0.25 to 1.75
- norm_bias: float32 [2, 2, 768], P('section'), may hold values from -1.75 to 1.75
- image_kv: bfloat16 [1024, 1536], P(None, 'section'), may hold values from -0.1875 to 0.1875
- cross_query: bfloat16 [768, 768], replicated, may hold values from -0.21875 to 0.21875
- cross_out: bfloat16 [768, 768], replicated, may hold values from -2.5 to 2.5
- cross_gain: float32 [768], replicated, may hold values from 0.25 to 1.75
- cross_bias: float32 [768], replicated, may hold values from -1.75 to 1.75
Outputs:
- layer_outputs: bfloat16 [2, 10240, 768], P('section', 'dp')
- input_grads: float32 [2, 10240, 768], P('section', 'dp')
- image_grad: float32 [256, 145, 1024], P('dp', None, 'section')
- grad_self_qkv: float32 [2, 768, 2304], P('section', 'dp')
- grad_self_out: float32 [2, 768, 768], P('section', 'dp')
- grad_ffn_up: float32 [2, 768, 3072], P('section', 'dp')
- grad_ffn_down: float32 [2, 3072, 768], P('section', 'dp')
- grad_norm_gain: float32 [2, 2, 768], P('section', None, 'dp')
- grad_norm_bias: float32 [2, 2, 768], P('section', None, 'dp')
- grad_image_kv: float32 [1024, 1536], P('dp', 'section')
- grad_cross_query: float32 [768, 768], P(None, ('section', 'dp'))
- grad_cross_out: float32 [768, 768], P(None, ('section', 'dp'))
- grad_cross_gain: float32 [768], P(('section', 'dp'))
- grad_cross_bias: float32 [768], P(('section', 'dp'))
Inputs may be any that keep to these rules, and one draw needn't show every extreme that they name: `segment_ids`: each row of 40 tokens holds 3 texts in order, each of 1 to 24 tokens, one of exactly 24. row_image[b] names each of the 4 images of rows b * 4 to (b + 1) * 4 - 1 once.
All inputs are finite; a program needn't handle non-finite values.
Results may differ from a plain program's by a relative error of at most 0.035.
Values may be sent and summed in bfloat16 or wider, within the bound.
A program may use at most 832 MiB of HBM per device.

v0:
```python
import math

import jax
import jax.numpy as jnp
from jax import lax
from jax.sharding import PartitionSpec as P

HEADS = 12


EPSILON = 1e-06
MASKED = -1e30


def from_behind(value, axis, steps):
    count = lax.axis_size(axis)
    first, last = (max(0, -steps), min(count, count - steps))
    return lax.ppermute(value, axis, [(source, source + steps) for source in range(first, last)])


def matmul(left, right):
    return jnp.dot(left, right, preferred_element_type=jnp.float32)


def dense_left(left, right):
    return lax.dot_general(
        left, right, (((0,), (0,)), ((), ())), preferred_element_type=jnp.float32
    )


def dense_right(left, right):
    return lax.dot_general(
        left, right, (((1,), (1,)), ((), ())), preferred_element_type=jnp.float32
    )


def norm_forward(summed, gain_vec, bias_vec):
    average = jnp.mean(summed, -1, keepdims=True)
    centred = summed - average
    variance = jnp.mean(centred * centred, -1, keepdims=True)
    inv_std = lax.rsqrt(variance + EPSILON)
    normed = centred * inv_std
    return (normed * gain_vec + bias_vec, (normed, inv_std))


def norm_backward(norm_kept, gain_vec, grad_out):
    normed, inv_std = norm_kept
    grad_gain = jnp.sum(grad_out * normed, 0)
    grad_bias = jnp.sum(grad_out, 0)
    grad_normed = grad_out * gain_vec
    grad_in = inv_std * (
        grad_normed
        - jnp.mean(grad_normed, -1, keepdims=True)
        - normed * jnp.mean(grad_normed * normed, -1, keepdims=True)
    )
    return (grad_in, grad_gain, grad_bias)


def gelu_value(preact):
    return 0.5 * preact * (1.0 + jax.scipy.special.erf(preact * math.sqrt(0.5)))


def gelu_slope(preact):
    return 0.5 * (1.0 + jax.scipy.special.erf(preact * math.sqrt(0.5))) + preact * jnp.exp(
        -0.5 * preact * preact
    ) / math.sqrt(2.0 * math.pi)


def split_heads(matrix, head_count):
    return matrix.reshape(matrix.shape[0], head_count, -1)


def scores_of(queries, key_rows, allowed, head_count):
    head_dim = queries.shape[1] // head_count
    scores = jnp.einsum(
        "qhd,khd->hqk",
        split_heads(queries, head_count),
        split_heads(key_rows, head_count),
        preferred_element_type=jnp.float32,
    )
    return jnp.where(allowed[None], scores * (1.0 / math.sqrt(head_dim)), MASKED)


def attend(queries, key_rows, value_rows, allowed, head_count):
    scores = scores_of(queries, key_rows, allowed, head_count)
    largest = jnp.max(scores, -1, keepdims=True)
    unnormed = jnp.exp(scores - largest)
    row_total = jnp.sum(unnormed, -1, keepdims=True)
    soft_weights = (unnormed / row_total).astype(jnp.bfloat16)
    attended = jnp.einsum(
        "hqk,khd->qhd",
        soft_weights,
        split_heads(value_rows, head_count),
        preferred_element_type=jnp.float32,
    )
    return (attended.reshape(queries.shape[0], -1), largest + jnp.log(row_total))


def attend_back(queries, key_rows, value_rows, allowed, log_total, grad_b, head_count):
    scores = scores_of(queries, key_rows, allowed, head_count)
    soft_weights = jnp.exp(scores - log_total)
    head_grad = split_heads(grad_b, head_count)
    grad_weights = jnp.einsum(
        "qhd,khd->hqk",
        head_grad,
        split_heads(value_rows, head_count),
        preferred_element_type=jnp.float32,
    )
    grad_scores = (
        soft_weights * (grad_weights - jnp.sum(grad_weights * soft_weights, -1, keepdims=True))
    ).astype(jnp.bfloat16)
    scaling = 1.0 / math.sqrt(queries.shape[1] // head_count)
    grad_query = (
        jnp.einsum(
            "hqk,khd->qhd",
            grad_scores,
            split_heads(key_rows, head_count),
            preferred_element_type=jnp.float32,
        )
        * scaling
    )
    grad_key = (
        jnp.einsum(
            "hqk,qhd->khd",
            grad_scores,
            split_heads(queries, head_count),
            preferred_element_type=jnp.float32,
        )
        * scaling
    )
    grad_value = jnp.einsum(
        "hqk,qhd->khd",
        soft_weights.astype(jnp.bfloat16),
        head_grad,
        preferred_element_type=jnp.float32,
    )
    return (
        grad_query.reshape(queries.shape[0], -1),
        grad_key.reshape(key_rows.shape[0], -1),
        grad_value.reshape(key_rows.shape[0], -1),
    )


def self_forward(residual, residual_b, w_qkv, w_out, gain_vec, bias_vec, allowed, head_count):
    projected = matmul(residual_b, w_qkv).astype(jnp.bfloat16)
    queries, key_rows, value_rows = jnp.split(projected, 3, axis=-1)
    attended, log_total = attend(queries, key_rows, value_rows, allowed, head_count)
    attended_b = attended.astype(jnp.bfloat16)
    normed_out, norm_kept = norm_forward(residual + matmul(attended_b, w_out), gain_vec, bias_vec)
    return (normed_out, (projected, log_total, attended_b, norm_kept))


def self_backward(grad_out, residual_b, w_qkv, w_out, gain_vec, saved, allowed, head_count):
    projected, log_total, attended_b, norm_kept = saved
    grad_sum, grad_gain, grad_bias = norm_backward(norm_kept, gain_vec, grad_out)
    branch_b = grad_sum.astype(jnp.bfloat16)
    grad_w_out = dense_left(attended_b, branch_b)
    grad_att = dense_right(branch_b, w_out).astype(jnp.bfloat16)
    queries, key_rows, value_rows = jnp.split(projected, 3, axis=-1)
    pieces = attend_back(queries, key_rows, value_rows, allowed, log_total, grad_att, head_count)
    grad_proj = jnp.concatenate(pieces, -1).astype(jnp.bfloat16)
    grad_w_qkv = dense_left(residual_b, grad_proj)
    grad_in = grad_sum + dense_right(grad_proj, w_qkv)
    return (grad_in, (grad_w_qkv, grad_w_out, grad_gain, grad_bias))


def ffn_forward(residual, w_up, w_down, gain_vec, bias_vec):
    residual_b = residual.astype(jnp.bfloat16)
    preact = matmul(residual_b, w_up)
    hidden_b = gelu_value(preact).astype(jnp.bfloat16)
    normed_out, norm_kept = norm_forward(residual + matmul(hidden_b, w_down), gain_vec, bias_vec)
    return (normed_out, (residual_b, preact, hidden_b, norm_kept))


def ffn_backward(grad_out, w_up, w_down, gain_vec, saved):
    residual_b, preact, hidden_b, norm_kept = saved
    grad_sum, grad_gain, grad_bias = norm_backward(norm_kept, gain_vec, grad_out)
    branch_b = grad_sum.astype(jnp.bfloat16)
    grad_w_down = dense_left(hidden_b, branch_b)
    grad_preact = (dense_right(branch_b, w_down) * gelu_slope(preact)).astype(jnp.bfloat16)
    grad_w_up = dense_left(residual_b, grad_preact)
    grad_in = grad_sum + dense_right(grad_preact, w_up)
    return (grad_in, (grad_w_up, grad_w_down, grad_gain, grad_bias))


def cross_forward(
    residual, key_rows, value_rows, w_query, w_out, gain_vec, bias_vec, allowed, head_count
):
    residual_b = residual.astype(jnp.bfloat16)
    queries = matmul(residual_b, w_query).astype(jnp.bfloat16)
    attended, log_total = attend(queries, key_rows, value_rows, allowed, head_count)
    attended_b = attended.astype(jnp.bfloat16)
    normed_out, norm_kept = norm_forward(residual + matmul(attended_b, w_out), gain_vec, bias_vec)
    return (normed_out, (residual_b, queries, log_total, attended_b, norm_kept))


def cross_backward(
    grad_out, key_rows, value_rows, w_query, w_out, gain_vec, saved, allowed, head_count
):
    residual_b, queries, log_total, attended_b, norm_kept = saved
    grad_sum, grad_gain, grad_bias = norm_backward(norm_kept, gain_vec, grad_out)
    branch_b = grad_sum.astype(jnp.bfloat16)
    grad_w_out = dense_left(attended_b, branch_b)
    grad_att = dense_right(branch_b, w_out).astype(jnp.bfloat16)
    grad_query, grad_key, grad_value = attend_back(
        queries, key_rows, value_rows, allowed, log_total, grad_att, head_count
    )
    grad_query = grad_query.astype(jnp.bfloat16)
    grad_w_query = dense_left(residual_b, grad_query)
    grad_in = grad_sum + dense_right(grad_query, w_query)
    return (
        grad_in,
        grad_key.astype(jnp.bfloat16),
        grad_value.astype(jnp.bfloat16),
        (grad_w_query, grad_w_out, grad_gain, grad_bias),
    )


def build_masks(segments, pictures, patches):
    row_count, length_row = segments.shape
    token_ids = (segments + length_row * jnp.arange(row_count, dtype=jnp.int32)[:, None]).reshape(
        -1
    )
    self_mask = token_ids[:, None] == token_ids[None, :]
    token_image = jnp.repeat(pictures, length_row)
    patch_image = jnp.arange(row_count * patches, dtype=jnp.int32) // patches
    return (self_mask, token_image[:, None] == patch_image[None, :])


def text_forward(params, tokens_b, self_mask, image_flat):
    w_qkv, w_out, w_up, w_down, gain_table, bias_table, w_img = params[:7]
    middle = self_forward(
        tokens_b.astype(jnp.float32),
        tokens_b,
        w_qkv,
        w_out,
        gain_table[0],
        bias_table[0],
        self_mask,
        HEADS,
    )[0]
    text_out = ffn_forward(middle, w_up, w_down, gain_table[1], bias_table[1])[0]
    return (text_out.astype(jnp.bfloat16), matmul(image_flat, w_img).astype(jnp.bfloat16))


def text_backward(params, tokens_b, self_mask, image_flat, grad_text_b, grad_key_b):
    w_qkv, w_out, w_up, w_down, gain_table, bias_table, w_img = params[:7]
    middle, self_kept = self_forward(
        tokens_b.astype(jnp.float32),
        tokens_b,
        w_qkv,
        w_out,
        gain_table[0],
        bias_table[0],
        self_mask,
        HEADS,
    )
    ffn_kept = ffn_forward(middle, w_up, w_down, gain_table[1], bias_table[1])[1]
    grad_middle, ffn_grads = ffn_backward(
        grad_text_b.astype(jnp.float32), w_up, w_down, gain_table[1], ffn_kept
    )
    grad_tokens, self_grads = self_backward(
        grad_middle, tokens_b, w_qkv, w_out, gain_table[0], self_kept, self_mask, HEADS
    )
    gradients = (
        self_grads[0],
        self_grads[1],
        ffn_grads[0],
        ffn_grads[1],
        jnp.stack([self_grads[2], ffn_grads[2]]),
        jnp.stack([self_grads[3], ffn_grads[3]]),
        dense_left(image_flat, grad_key_b),
    ) + tuple((jnp.zeros(tensor.shape, jnp.float32) for tensor in params[7:]))
    return (gradients, grad_tokens, dense_right(grad_key_b, w_img))


def joining_step(params, boundary_b, key_b, image_flat, self_mask, cross_mask, grad_joined):
    (
        w_qkv,
        w_out,
        w_up,
        w_down,
        gain_table,
        bias_table,
        w_img,
        w_query,
        w_cross,
        cross_gains,
        cross_shift,
    ) = params
    value_b = matmul(image_flat, w_img).astype(jnp.bfloat16)
    middle, self_kept = self_forward(
        boundary_b.astype(jnp.float32),
        boundary_b,
        w_qkv,
        w_out,
        gain_table[0],
        bias_table[0],
        self_mask,
        HEADS,
    )
    crossed, cross_kept = cross_forward(
        middle, key_b, value_b, w_query, w_cross, cross_gains, cross_shift, cross_mask, HEADS
    )
    joined_out, ffn_kept = ffn_forward(crossed, w_up, w_down, gain_table[1], bias_table[1])
    grad_crossed, ffn_grads = ffn_backward(
        grad_joined.astype(jnp.float32), w_up, w_down, gain_table[1], ffn_kept
    )
    grad_middle, grad_key_b, grad_value_b, cross_grads = cross_backward(
        grad_crossed, key_b, value_b, w_query, w_cross, cross_gains, cross_kept, cross_mask, HEADS
    )
    grad_boundary, self_grads = self_backward(
        grad_middle, boundary_b, w_qkv, w_out, gain_table[0], self_kept, self_mask, HEADS
    )
    gradients = (
        self_grads[0],
        self_grads[1],
        ffn_grads[0],
        ffn_grads[1],
        jnp.stack([self_grads[2], ffn_grads[2]]),
        jnp.stack([self_grads[3], ffn_grads[3]]),
        dense_left(image_flat, grad_value_b),
    ) + cross_grads
    return (
        gradients,
        joined_out.astype(jnp.bfloat16),
        grad_boundary,
        grad_boundary.astype(jnp.bfloat16),
        grad_key_b,
        dense_right(grad_value_b, w_img),
    )


def per_device(
    text_in,
    cotangent,
    images,
    segment_ids,
    row_image,
    self_qkv,
    self_out,
    ffn_up,
    ffn_down,
    norm_gain,
    norm_bias,
    image_kv,
    cross_query,
    cross_out,
    cross_gain,
    cross_bias,
):
    params = (
        self_qkv[0],
        self_out[0],
        ffn_up[0],
        ffn_down[0],
        norm_gain[0],
        norm_bias[0],
        image_kv,
        cross_query,
        cross_out,
        cross_gain,
        cross_bias,
    )
    micro_count, rows_micro = row_image.shape
    length_row = segment_ids.shape[1]
    patches = images.shape[1]
    image_width = images.shape[2]
    tokens_micro = rows_micro * length_row
    model_width = text_in.shape[1]
    token_shape = (tokens_micro, model_width)
    key_shape = (rows_micro * patches, model_width)
    part_shape = (rows_micro * patches, image_width)
    is_text = lax.axis_index("section") == 0
    zero_grads = tuple((jnp.zeros(tensor.shape, jnp.float32) for tensor in params))

    def inputs_of(micro_index):
        first_tok = micro_index * tokens_micro
        first_row = micro_index * rows_micro
        segments = segment_ids[first_row : first_row + rows_micro]
        self_mask, cross_mask = build_masks(segments, row_image[micro_index], patches)
        image_flat = images[first_row : first_row + rows_micro].reshape(
            rows_micro * patches, image_width
        )
        return (
            text_in[first_tok : first_tok + tokens_micro],
            cotangent[first_tok : first_tok + tokens_micro],
            image_flat,
            self_mask,
            cross_mask,
        )

    def run_joining(micro_index, boundary_b, key_b):
        tokens_b, grad_joined, image_flat, self_mask, cross_mask = inputs_of(micro_index)

        def skipped():
            return (
                zero_grads,
                jnp.zeros(token_shape, jnp.bfloat16),
                jnp.zeros(token_shape, jnp.float32),
                jnp.zeros(token_shape, jnp.bfloat16),
                jnp.zeros(key_shape, jnp.bfloat16),
                jnp.zeros(part_shape, jnp.float32),
            )

        return lax.cond(
            is_text,
            skipped,
            lambda: joining_step(
                params, boundary_b, key_b, image_flat, self_mask, cross_mask, grad_joined
            ),
        )

    def run_text_back(micro_index, grad_text_b, grad_key_b):
        tokens_b, grad_joined, image_flat, self_mask, cross_mask = inputs_of(micro_index)

        def skipped():
            return (
                zero_grads,
                jnp.zeros(token_shape, jnp.float32),
                jnp.zeros(part_shape, jnp.float32),
            )

        return lax.cond(
            is_text,
            lambda: text_backward(params, tokens_b, self_mask, image_flat, grad_text_b, grad_key_b),
            skipped,
        )

    def settle(gradients, totals):
        full_sum, shard_sum, cross_sum = totals
        cross_sum = tuple((running + addend for running, addend in zip(cross_sum, gradients[7:])))
        full_sum = tuple((running + addend for running, addend in zip(full_sum, gradients[:7])))
        return (full_sum, shard_sum, cross_sum)

    totals = (zero_grads[:7], None, zero_grads[7:])
    text_outs, joined_outs, joining_grads, joining_parts = ([], [], [], [])
    text_grads, text_parts, sent_back = ([], [], [])
    for micro_index in range(micro_count):
        run_tokens_b, run_grad_joined, run_image_flat, run_self_mask, run_cross_mask = inputs_of(
            micro_index
        )

        def run_skipped():
            return (jnp.zeros(token_shape, jnp.bfloat16), jnp.zeros(key_shape, jnp.bfloat16))

        text_out_b, key_b = lax.cond(
            is_text,
            lambda: text_forward(params, run_tokens_b, run_self_mask, run_image_flat),
            run_skipped,
        )
        text_outs.append(text_out_b)
        boundary_b, got_key_b = from_behind((text_out_b, key_b), "section", 1)
        gradients, joined_b, grad_boundary, grad_boundary_b, grad_key_b, image_part = run_joining(
            micro_index, boundary_b, got_key_b
        )
        totals = settle(gradients, totals)
        joined_outs.append(joined_b)
        joining_grads.append(grad_boundary)
        joining_parts.append(image_part)
        sent_back.append((grad_boundary_b, grad_key_b))
    returned_text, returned_key = from_behind(
        (
            jnp.stack([sent_pair[0] for sent_pair in sent_back]),
            jnp.stack([sent_pair[1] for sent_pair in sent_back]),
        ),
        "section",
        -1,
    )
    for micro_index in range(micro_count):
        back_grad_text_b = returned_text[micro_index]
        back_grad_key_b = returned_key[micro_index]
        back_gradients, grad_tokens, back_image_part = run_text_back(
            micro_index, back_grad_text_b, back_grad_key_b
        )
        totals, grad_tokens, image_part = (
            settle(back_gradients, totals),
            grad_tokens,
            back_image_part,
        )
        text_grads.append(grad_tokens)
        text_parts.append(image_part)
    full_sum, shard_sum, cross_sum = totals
    shard_sum = (
        lax.psum_scatter(full_sum[0], "dp", scatter_dimension=0, tiled=True),
        lax.psum_scatter(full_sum[1], "dp", scatter_dimension=0, tiled=True),
        lax.psum_scatter(full_sum[2], "dp", scatter_dimension=0, tiled=True),
        lax.psum_scatter(full_sum[3], "dp", scatter_dimension=0, tiled=True),
        lax.psum_scatter(full_sum[4], "dp", scatter_dimension=1, tiled=True),
        lax.psum_scatter(full_sum[5], "dp", scatter_dimension=1, tiled=True),
        lax.psum_scatter(full_sum[6], "dp", scatter_dimension=0, tiled=True),
    )
    cross_shards = (
        lax.psum_scatter(cross_sum[0], ("section", "dp"), scatter_dimension=1, tiled=True),
        lax.psum_scatter(cross_sum[1], ("section", "dp"), scatter_dimension=1, tiled=True),
        lax.psum_scatter(cross_sum[2], ("section", "dp"), scatter_dimension=0, tiled=True),
        lax.psum_scatter(cross_sum[3], ("section", "dp"), scatter_dimension=0, tiled=True),
    )
    image_parts = jnp.concatenate(
        [
            joining_piece + text_piece
            for joining_piece, text_piece in zip(joining_parts, text_parts)
        ],
        0,
    )
    image_grad = lax.psum_scatter(
        image_parts.reshape(micro_count * rows_micro, patches, image_width).astype(jnp.bfloat16),
        "section",
        scatter_dimension=2,
        tiled=True,
    ).astype(jnp.float32)
    layer_outputs = jnp.where(
        is_text, jnp.concatenate(text_outs, 0), jnp.concatenate(joined_outs, 0)
    )[None]
    input_grads = jnp.where(
        is_text, jnp.concatenate(text_grads, 0), jnp.concatenate(joining_grads, 0)
    )[None]
    return (
        layer_outputs,
        input_grads,
        image_grad,
        shard_sum[0][None],
        shard_sum[1][None],
        shard_sum[2][None],
        shard_sum[3][None],
        shard_sum[4][None],
        shard_sum[5][None],
        shard_sum[6],
        cross_shards[0],
        cross_shards[1],
        cross_shards[2],
        cross_shards[3],
    )


def solution(mesh):
    return jax.shard_map(
        per_device,
        mesh=mesh,
        in_specs=(
            P("dp", None),
            P("dp", None),
            P("dp", None, None),
            P("dp", None),
            P("dp", None),
            P("section", None, None),
            P("section", None, None),
            P("section", None, None),
            P("section", None, None),
            P("section", None, None),
            P("section", None, None),
            P(None, "section"),
            P(),
            P(),
            P(),
            P(),
        ),
        out_specs=(
            P("section", "dp", None),
            P("section", "dp", None),
            P("dp", None, "section"),
            P("section", "dp", None),
            P("section", "dp", None),
            P("section", "dp", None),
            P("section", "dp", None),
            P("section", None, "dp"),
            P("section", None, "dp"),
            P("dp", "section"),
            P(None, ("section", "dp")),
            P(None, ("section", "dp")),
            P(("section", "dp")),
            P(("section", "dp")),
        ),
        check_vma=False,
    )
```

profile of v0, /device:TPU:0, one launch (start us, length us, event | category | flops | bytes accessed | tf_op | source)
XLA Modules:
  0.0 2047.7 jit_solution(15431250315121565769)
XLA Ops:
  11.8 6.0 fusion.547
  22.1 34.0 %conditional.15 = (bf16[160,768]{1,0:T(8,128)(2,1)}, bf16[580,768]{1,0:T(8,128)(2,1)}, bf16[1,160,768]{2,1,0:T(8,128)(2,1)}) conditional(s32[]{:T(128)} %convert_element_type.861, () %tuple.174, (bf16[160,768]{1,0:T(8,128)(2,1)}, bf16[768,2304]{1,0:T(8,128)(2,1)S(1)}, pred[160,160]{0,1:T(8,128)(4,1)}, bf16[768,768]{1,0:T(8,128)(2,1)}, ...), branch_computations={%region_24.25_spmd, %region_25.32_spmd} | conditional | flops 3264753152 | bytes 37371016 | solution.py:447
  43.0 7.4 fusion.504
  66.5 34.2 %conditional.12 = (bf16[160,768]{1,0:T(8,128)(2,1)}, bf16[580,768]{1,0:T(8,128)(2,1)}, bf16[1,160,768]{2,1,0:T(8,128)(2,1)}) conditional(s32[]{:T(128)} %convert_element_type.861, () %tuple.168, (bf16[160,768]{1,0:T(8,128)(2,1)}, bf16[768,2304]{1,0:T(8,128)(2,1)S(1)}, pred[160,160]{0,1:T(8,128)(4,1)}, bf16[768,768]{1,0:T(8,128)(2,1)}, ...), branch_computations={%region_0.0_spmd, %region_1.8_spmd} | conditional | flops 3264753152 | bytes 37371016 | solution.py:447
  87.5 7.4 fusion.486
  111.0 34.2 %conditional.13 = (bf16[160,768]{1,0:T(8,128)(2,1)}, bf16[580,768]{1,0:T(8,128)(2,1)}, bf16[1,160,768]{2,1,0:T(8,128)(2,1)}) conditional(s32[]{:T(128)} %convert_element_type.861, () %tuple.170, (bf16[160,768]{1,0:T(8,128)(2,1)}, bf16[768,2304]{1,0:T(8,128)(2,1)S(1)}, pred[160,160]{0,1:T(8,128)(4,1)}, bf16[768,768]{1,0:T(8,128)(2,1)}, ...), branch_computations={%region_8.9_spmd, %region_9.16_spmd} | conditional | flops 3264753152 | bytes 37395648 | solution.py:447
  132.1 7.4 fusion.492
  154.2 34.4 %conditional.14 = (bf16[160,768]{1,0:T(8,128)(2,1)}, bf16[580,768]{1,0:T(8,128)(2,1)}, bf16[1,160,768]{2,1,0:T(8,128)(2,1)S(1)}) conditional(s32[]{:T(128)} %convert_element_type.861, () %tuple.172, (bf16[160,768]{1,0:T(8,128)(2,1)}, bf16[768,2304]{1,0:T(8,128)(2,1)S(1)}, pred[160,160]{0,1:T(8,128)(4,1)}, bf16[768,768]{1,0:T(8,128)(2,1)}, ...), branch_computations={%region_16.17_spmd, %region_17.24_spmd} | conditional | flops 3264753152 | bytes 37371016 | solution.py:447
  176.1 7.4 fusion.498
  192.7 22.7 %collective-permute-done.2 = bf16[160,768]{1,0:T(8,128)(2,1)} collective-permute-done((bf16[160,768]{1,0:T(8,128)(2,1)}, bf16[160,768]{1,0:T(8,128)(2,1)}, u32[]{:S(2)}, u32[]{:S(2)}) %collective-permute-start.2) | collective-permute-done | bytes 245792 | tf_op jit(solution)/shard_map/ppermute | solution.py:18
  215.4 5.1 collective-permute-start
  233.2 24.1 %conditional.16 = (f32[768,768]{1,0:T(8,128)}, f32[768,3072]{1,0:T(8,128)S(1)}, f32[3072,768]{1,0:T(8,128)S(1)}, f32[2,768]{1,0:T(2,128)}, f32[2,768]{1,0:T(2,12...) conditional(s32[]{:T(128)} %convert_element_type.861, ...), branch_computations={%region_32.57_spmd, %region_57.58_spmd} | conditional | flops 11812423680 | bytes 377501504 | solution.py:406
  263.8 23.8 %conditional.17 = (f32[768,768]{1,0:T(8,128)}, f32[768,3072]{1,0:T(8,128)S(1)}, f32[3072,768]{1,0:T(8,128)S(1)}, f32[2,768]{1,0:T(2,128)}, f32[2,768]{1,0:T(2,12...) conditional(s32[]{:T(128)} %convert_element_type.861, ...), branch_computations={%region_58.83_spmd, %region_83.84_spmd} | conditional | flops 11812423680 | bytes 377501504 | solution.py:406
  294.2 24.2 %conditional.19 = (f32[768,768]{1,0:T(8,128)}, f32[768,3072]{1,0:T(8,128)S(1)}, f32[3072,768]{1,0:T(8,128)S(1)}, f32[2,768]{1,0:T(2,128)}, f32[2,768]{1,0:T(2,12...) conditional(s32[]{:T(128)} %convert_element_type.861, ...), branch_computations={%region_110.135_spmd, %region_135.136_spmd} | conditional | flops 11812423680 | bytes 377501504 | solution.py:406
  324.8 26.7 %conditional.18 = (f32[768,768]{1,0:T(8,128)}, f32[768,3072]{1,0:T(8,128)S(1)}, f32[3072,768]{1,0:T(8,128)S(1)}, f32[2,768]{1,0:T(2,128)}, f32[2,768]{1,0:T(2,12...) conditional(s32[]{:T(128)} %convert_element_type.861, ...), branch_computations={%region_84.109_spmd, %region_109.110_spmd} | conditional | flops 11812423680 | bytes 377501504 | solution.py:406
  351.6 12.1 pad_maximum_fusion.40
  366.5 498.1 %collective-permute-done.8 = bf16[4,160,768]{2,1,0:T(8,128)(2,1)} collective-permute-done((bf16[4,160,768]{2,1,0:T(8,128)(2,1)S(1)}, bf16[4,160,768]{2,1,0:T(8,128)(2,1)}, u32[]{:S(2)}, u32[]{:S(2)}) %collective-permute-start.8) | collective-permute-done | bytes 983072 | tf_op jit(solution)/shard_map/ppermute | solution.py:18
  864.7 75.0 %conditional.20 = (f32[768,768]{1,0:T(8,128)}, f32[768,3072]{1,0:T(8,128)}, f32[3072,768]{1,0:T(8,128)}, f32[2,768]{1,0:T(2,128)}, f32[2,768]{1,0:T(2,128)}, /*i...) conditional(s32[]{:T(128)} %convert_element_type.861, ...), branch_computations={%region_136.137_spmd.clone, %region_137.153_spmd.clone} | conditional | flops 8886003712 | bytes 225045264 | solution.py:424
  919.1 8.0 copy.533
  927.1 7.1 fusion.355
  934.2 5.2 fusion.360
  939.6 83.4 %conditional.21 = (f32[768,768]{1,0:T(8,128)}, f32[768,3072]{1,0:T(8,128)}, f32[3072,768]{1,0:T(8,128)}, f32[2,768]{1,0:T(2,128)}, f32[2,768]{1,0:T(2,128)}, /*i...) conditional(s32[]{:T(128)} %convert_element_type.861, ...), branch_computations={%region_153.154_spmd.clone, %region_154.170_spmd.clone} | conditional | flops 8886003712 | bytes 225045264 | solution.py:424
  1002.3 8.1 copy.535
  1010.4 7.0 fusion.393
  1017.5 5.1 fusion.398
  1023.1 83.0 %conditional.22 = (f32[768,768]{1,0:T(8,128)}, f32[768,3072]{1,0:T(8,128)}, f32[3072,768]{1,0:T(8,128)}, f32[2,768]{1,0:T(2,128)}, f32[2,768]{1,0:T(2,128)}, /*i...) conditional(s32[]{:T(128)} %convert_element_type.861, ...), branch_computations={%region_170.171_spmd.clone, %region_171.187_spmd.clone} | conditional | flops 8886003712 | bytes 225045264 | solution.py:424
  1085.6 8.0 copy.537
  1093.6 7.0 fusion.431
  1100.7 5.2 fusion.436
  1106.1 82.4 %conditional.23 = (f32[768,768]{1,0:T(8,128)}, f32[768,3072]{1,0:T(8,128)}, f32[3072,768]{1,0:T(8,128)}, f32[2,768]{1,0:T(2,128)}, f32[2,768]{1,0:T(2,128)}, /*i...) conditional(s32[]{:T(128)} %convert_element_type.861, ...), branch_computations={%region_187.188_spmd.clone, %region_188.204_spmd.clone} | conditional | flops 8886003712 | bytes 234865104 | solution.py:424
  1168.5 8.2 copy.539
  1176.8 6.4 fusion.469
  1201.4 21.8 %concatenate.148 = bf16[2320,1024]{1,0:T(8,128)(2,1)} concatenate(bf16[580,1024]{1,0:T(8,128)(2,1)S(1)} %get-tuple-element.1603, bf16[580,1024]{1,0:T(8,128)(2,1)S(1)} %get-tuple-element.1602, bf16[580,1024]{1,0:T(8,128)(2,1)} %get-tuple-element.1601, bf16[580,1024]{1,0:T(8,128)(2,1)} %get-tuple-element.1600), dimensions={0} | concatenate | bytes 9502720 | tf_op jit(solution)/shard_map/concatenate | solution.py:499
  1229.5 5.1 add_add_fusion.4
  1236.2 5.1 add_add_fusion.5
  1241.4 9.3 add_add_fusion.6
  1250.8 10.7 add_add_fusion.3
  1261.5 21.8 %add_add_fusion.2 = f32[768,2304]{1,0:T(8,128)} fusion(f32[768,2304]{1,0:T(8,128)} %get-tuple-element.1281, f32[768,2304]{1,0:T(8,128)} %get-tuple-element.1280, f32[768,2304]{1,0:T(8,128)} %get-tuple-element.1279, f32[768,2304]{1,0:T(8,128)} %get-tuple-element.1278, f32[768,2304]{1,0:T(8,128)} %get-tuple-element.1274, f32[768,2304]{1,0:T(8,128)} %get-tuple-element.1269, ...), kind=kLoop, calls=%fused_computation.974 | loop fusion | flops 12386304 | bytes 63700992 | tf_op jit(solution)/shard_map/add | solution.py:433
  1283.4 28.5 %add_add_fusion = f32[3072,768]{1,0:T(8,128)} fusion(f32[3072,768]{1,0:T(8,128)} %get-tuple-element.974, f32[3072,768]{1,0:T(8,128)} %get-tuple-element.963, f32[3072,768]{1,0:T(8,128)} %get-tuple-element.952, f32[3072,768]{1,0:T(8,128)} %get-tuple-element.941, f32[3072,768]{1,0:T(8,128)} %copy-done.35, f32[3072,768]{1,0:T(8,128)} %copy-done.36, ...), kind=kLoop, calls=%fused_computation.972 | loop fusion | flops 16515072 | bytes 84934656 | tf_op jit(solution)/shard_map/add | solution.py:433
  1312.2 30.8 %add_add_fusion.1 = f32[768,3072]{1,0:T(8,128)} fusion(f32[768,3072]{1,0:T(8,128)} %get-tuple-element.973, f32[768,3072]{1,0:T(8,128)} %get-tuple-element.962, f32[768,3072]{1,0:T(8,128)} %get-tuple-element.951, f32[768,3072]{1,0:T(8,128)} %get-tuple-element.940, f32[768,3072]{1,0:T(8,128)} %copy-done.39, f32[768,3072]{1,0:T(8,128)} %copy-done.40, ...), kind=kLoop, calls=%fused_computation.973 | loop fusion | flops 16515072 | bytes 84934656 | tf_op jit(solution)/shard_map/add | solution.py:433
  1346.8 39.7 %all-reduce.2 = (f32[768]{0:T(1024)S(1)}, f32[768]{0:T(1024)S(1)}) all-reduce(f32[768]{0:T(1024)S(1)} %get-tuple-element.1599, f32[768]{0:T(1024)S(1)} %get-tuple-element.1598), channel_id=12, replica_groups=mesh['section'=2,'dp'=16] {'section','dp'}, use_global_device_ids=true, to_apply=%region_214.215.clone | all-reduce | flops 1536 | bytes 12288
  1398.2 76.8 %reduce-scatter.29.cloned.1.call-done = f32[768,24]{0,1:T(8,128)} async-done(((f32[768,768]{0,1:T(8,128)}), f32[768,24]{0,1:T(8,128)}) %reduce-scatter.29.cloned.1.call-update) | async-done | bytes 73744 | tf_op jit(solution)/shard_map/reduce_scatter | solution.py:495
  1474.9 103.9 %reduce-scatter.27.cloned.1.call-done = f32[768,24]{0,1:T(8,128)} async-done(((f32[768,768]{0,1:T(8,128)}), f32[768,24]{0,1:T(8,128)}) %reduce-scatter.27.cloned.1.call-update) | async-done | bytes 73744 | tf_op jit(solution)/shard_map/reduce_scatter | solution.py:494
  1578.8 66.6 %reduce-scatter.19.cloned.1.call-done = f32[48,768]{1,0:T(8,128)} async-done(((f32[768,768]{1,0:T(8,128)}), f32[48,768]{1,0:T(8,128)}) %reduce-scatter.19.cloned.1.call-update) | async-done | bytes 147472 | tf_op jit(solution)/shard_map/reduce_scatter | solution.py:486
  1645.5 69.7 %reduce-scatter.25.cloned.1.call-done = f32[64,768]{1,0:T(8,128)} async-done(((f32[1024,768]{1,0:T(8,128)}), f32[64,768]{1,0:T(8,128)}) %reduce-scatter.25.cloned.1.call-update) | async-done | bytes 196624 | tf_op jit(solution)/shard_map/reduce_scatter | solution.py:491
  1715.1 93.7 %reduce-scatter.17.cloned.1.call-done = f32[48,2304]{1,0:T(8,128)} async-done(((f32[768,2304]{1,0:T(8,128)}), f32[48,2304]{1,0:T(8,128)}) %reduce-scatter.17.cloned.1.call-update) | async-done | bytes 442384 | tf_op jit(solution)/shard_map/reduce_scatter | solution.py:485
  1808.8 116.1 %reduce-scatter.23.cloned.1.call-done = f32[192,768]{1,0:T(8,128)} async-done(((f32[3072,768]{1,0:T(8,128)}), f32[192,768]{1,0:T(8,128)}) %reduce-scatter.23.cloned.1.call-update) | async-done | bytes 589840 | tf_op jit(solution)/shard_map/reduce_scatter | solution.py:488
  1924.9 115.7 %reduce-scatter.21.cloned.1.call-done = f32[48,3072]{1,0:T(8,128)} async-done(((f32[768,3072]{1,0:T(8,128)}), f32[48,3072]{1,0:T(8,128)}) %reduce-scatter.21.cloned.1.call-update) | async-done | bytes 589840 | tf_op jit(solution)/shard_map/reduce_scatter | solution.py:487
  (855 shorter events, 520.5 us)
Async XLA Ops:
  7.2 1383.5 %reduce-scatter.33.cloned.1.call-start = ((), (), s32[]{:S(2)}) async-start(), calls=%async_computation.19 | async-start | bytes 417792
  56.1 231.5 %collective-permute-start.7 = (bf16[580,768]{1,0:T(8,128)(2,1)}, bf16[580,768]{1,0:T(8,128)(2,1)}, u32[]{:S(2)}, u32[]{:S(2)}) collective-permute-start(bf16[580,768]{1,0:T(8,128)(2,1)} %get-tuple-element.832), channel_id=1, source_target_pairs={{0,16},{1,17},{2,18},{3,19},{4,20},{5,21},{6,22},{7,23},{8,24},{9,... | collective-permute-start | bytes 2672648 | tf_op jit(solution)/shard_map/ppermute | solution.py:18
  100.6 129.8 %collective-permute-start.1 = (bf16[580,768]{1,0:T(8,128)(2,1)}, bf16[580,768]{1,0:T(8,128)(2,1)}, u32[]{:S(2)}, u32[]{:S(2)}) collective-permute-start(bf16[580,768]{1,0:T(8,128)(2,1)} %get-tuple-element.823), channel_id=1, source_target_pairs={{0,16},{1,17},{2,18},{3,19},{4,20},{5,21},{6,22},{7,23},{8,24},{9,... | collective-permute-start | bytes 2672648 | tf_op jit(solution)/shard_map/ppermute | solution.py:18
  132.1 9.3 copy-start.371
  145.2 112.1 %collective-permute-start.3 = (bf16[580,768]{1,0:T(8,128)(2,1)}, bf16[580,768]{1,0:T(8,128)(2,1)}, u32[]{:S(2)}, u32[]{:S(2)}) collective-permute-start(bf16[580,768]{1,0:T(8,128)(2,1)} %get-tuple-element.826), channel_id=1, source_target_pairs={{0,16},{1,17},{2,18},{3,19},{4,20},{5,21},{6,22},{7,23},{8,24},{9,... | collective-permute-start | bytes 2672648 | tf_op jit(solution)/shard_map/ppermute | solution.py:18
  154.2 79.1 %copy-start.192 = (f32[768]{0:T(1024)S(1)}, f32[768]{0:T(1024)}, u32[]{:S(2)}) copy-start(f32[768]{0:T(1024)} %param.54) | copy-start | bytes 9220
  154.2 79.1 %copy-start.205 = (f32[768]{0:T(1024)S(1)}, f32[768]{0:T(1024)}, u32[]{:S(2)}) copy-start(f32[768]{0:T(1024)} %param.55) | copy-start | bytes 9220
  188.5 44.7 %copy-start.270 = (bf16[1,160,768]{2,1,0:T(8,128)(2,1)}, bf16[1,160,768]{2,1,0:T(8,128)(2,1)S(1)}, u32[]{:S(2)}) copy-start(bf16[1,160,768]{2,1,0:T(8,128)(2,1)S(1)} %get-tuple-element.820) | copy-start | bytes 737284
  188.5 129.9 %collective-permute-start.5 = (bf16[580,768]{1,0:T(8,128)(2,1)}, bf16[580,768]{1,0:T(8,128)(2,1)}, u32[]{:S(2)}, u32[]{:S(2)}) collective-permute-start(bf16[580,768]{1,0:T(8,128)(2,1)} %get-tuple-element.829), channel_id=1, source_target_pairs={{0,16},{1,17},{2,18},{3,19},{4,20},{5,21},{6,22},{7,23},{8,24},{9,... | collective-permute-start | bytes 2672648 | tf_op jit(solution)/shard_map/ppermute | solution.py:18
  190.7 24.7 %collective-permute-start.2 = (bf16[160,768]{1,0:T(8,128)(2,1)}, bf16[160,768]{1,0:T(8,128)(2,1)}, u32[]{:S(2)}, u32[]{:S(2)}) collective-permute-start(bf16[160,768]{1,0:T(8,128)(2,1)} %get-tuple-element.825), channel_id=1, source_target_pairs={{0,16},{1,17},{2,18},{3,19},{4,20},{5,21},{6,22},{7,23},{8,24},{9,... | collective-permute-start | bytes 737288 | tf_op jit(solution)/shard_map/ppermute | solution.py:18
  215.4 9.9 collective-permute-start
  225.4 62.2 %collective-permute-start.6 = (bf16[160,768]{1,0:T(8,128)(2,1)}, bf16[160,768]{1,0:T(8,128)(2,1)}, u32[]{:S(2)}, u32[]{:S(2)}) collective-permute-start(bf16[160,768]{1,0:T(8,128)(2,1)} %get-tuple-element.831), channel_id=1, source_target_pairs={{0,16},{1,17},{2,18},{3,19},{4,20},{5,21},{6,22},{7,23},{8,24},{9,... | collective-permute-start | bytes 737288 | tf_op jit(solution)/shard_map/ppermute | solution.py:18
  230.4 88.0 %collective-permute-start.4 = (bf16[160,768]{1,0:T(8,128)(2,1)}, bf16[160,768]{1,0:T(8,128)(2,1)}, u32[]{:S(2)}, u32[]{:S(2)}) collective-permute-start(bf16[160,768]{1,0:T(8,128)(2,1)} %get-tuple-element.828), channel_id=1, source_target_pairs={{0,16},{1,17},{2,18},{3,19},{4,20},{5,21},{6,22},{7,23},{8,24},{9,... | collective-permute-start | bytes 737288 | tf_op jit(solution)/shard_map/ppermute | solution.py:18
  351.6 12.1 copy-start.36
  351.6 13.6 copy-start.40
  351.6 13.4 copy-start.266
  351.6 13.4 copy-start.267
  351.6 13.4 copy-start.268
  351.6 13.4 copy-start.269
  363.7 500.9 %copy-start.294 = (f32[1,2,768]{2,1,0:T(2,128)S(1)}, f32[1,2,768]{2,1,0:T(2,128)}, u32[]{:S(2)}) copy-start(f32[1,2,768]{2,1,0:T(2,128)} %param.50) | copy-start | bytes 18436
  363.7 500.9 %collective-permute-start.9 = (bf16[4,580,768]{2,0,1:T(4,128)(2,1)S(1)}, bf16[4,580,768]{2,0,1:T(4,128)(2,1)}, u32[]{:S(2)}, u32[]{:S(2)}) collective-permute-start(bf16[4,580,768]{2,0,1:T(4,128)(2,1)S(1)} %pad_maximum_fusion.40), channel_id=1, source_target_pairs={{16,0},{17,1},{18,2},{19,3},{20,4},{21,5},{22,6},{23,7},{24,8},{25... | collective-permute-start | bytes 10690568 | tf_op jit(solution)/shard_map/ppermute | solution.py:18
  365.2 499.4 %collective-permute-start.8 = (bf16[4,160,768]{2,1,0:T(8,128)(2,1)S(1)}, bf16[4,160,768]{2,1,0:T(8,128)(2,1)}, u32[]{:S(2)}, u32[]{:S(2)}) collective-permute-start(bf16[4,160,768]{2,1,0:T(8,128)(2,1)S(1)} %pad_maximum_fusion.41), channel_id=1, source_target_pairs={{16,0},{17,1},{18,2},{19,3},{20,4},{21,5},{22,6},{23,7},{24,8},{25... | collective-permute-start | bytes 2949128 | tf_op jit(solution)/shard_map/ppermute | solution.py:18
  880.9 12.2 copy-start.81
  880.9 12.2 copy-start.401
  881.2 11.9 copy-start.417
  964.0 12.2 copy-start.83
  964.0 12.2 copy-start.403
  964.3 11.9 copy-start.419
  1047.4 12.2 copy-start.85
  1047.4 12.2 copy-start.405
  1047.7 11.9 copy-start.421
  1130.1 12.3 copy-start.87
  1130.1 12.3 copy-start.407
  1130.5 11.9 copy-start.423
  1190.3 201.8 %reduce-scatter.31.cloned.1.call-start = ((), (), s32[]{:S(2)}) async-start(), calls=%async_computation.18 | async-start | bytes 417792
  1191.3 202.1 %reduce-scatter.15.cloned.1.call-start = ((), (), s32[]{:S(2)}) async-start(), calls=%async_computation.10 | async-start | bytes 7471104 | tf_op jit(solution)/shard_map/reduce_scatter | solution.py:506
  1227.8 247.1 %reduce-scatter.29.cloned.1.call-start = ((), (), s32[]{:S(2)}) async-start(), calls=%async_computation.17 | async-start | bytes 2433024 | tf_op jit(solution)/shard_map/reduce_scatter | solution.py:495
  1234.6 344.2 %reduce-scatter.27.cloned.1.call-start = ((), (), s32[]{:S(2)}) async-start(), calls=%async_computation.16 | async-start | bytes 2433024 | tf_op jit(solution)/shard_map/reduce_scatter | solution.py:494
  1241.4 404.1 %reduce-scatter.19.cloned.1.call-start = ((), (), s32[]{:S(2)}) async-start(), calls=%async_computation.12 | async-start | bytes 2506752 | tf_op jit(solution)/shard_map/reduce_scatter | solution.py:486
  1241.4 9.3 copy-start.89
  1250.7 464.4 %reduce-scatter.25.cloned.1.call-start = ((), (), s32[]{:S(2)}) async-start(), calls=%async_computation.15 | async-start | bytes 3342336 | tf_op jit(solution)/shard_map/reduce_scatter | solution.py:491
  1261.5 547.3 %reduce-scatter.17.cloned.1.call-start = ((), (), s32[]{:S(2)}) async-start(), calls=%async_computation.11 | async-start | bytes 7520256 | tf_op jit(solution)/shard_map/reduce_scatter | solution.py:485
  1283.3 641.6 %reduce-scatter.23.cloned.1.call-start = ((), (), s32[]{:S(2)}) async-start(), calls=%async_computation.14 | async-start | bytes 10027008 | tf_op jit(solution)/shard_map/reduce_scatter | solution.py:488
  1311.9 728.7 %reduce-scatter.21.cloned.1.call-start = ((), (), s32[]{:S(2)}) async-start(), calls=%async_computation.13 | async-start | bytes 10027008 | tf_op jit(solution)/shard_map/reduce_scatter | solution.py:487
  1343.1 44.5 %copy-start.194 = (f32[1,160,768]{2,1,0:T(8,128)S(1)}, f32[1,160,768]{2,1,0:T(8,128)}, u32[]{:S(2)}) copy-start(f32[1,160,768]{2,1,0:T(8,128)} %get-tuple-element.846) | copy-start | bytes 1474564
  1343.2 44.5 %copy-start.196 = (f32[1,160,768]{2,1,0:T(8,128)S(1)}, f32[1,160,768]{2,1,0:T(8,128)}, u32[]{:S(2)}) copy-start(f32[1,160,768]{2,1,0:T(8,128)} %get-tuple-element.847) | copy-start | bytes 1474564
  1343.2 44.5 %copy-start.198 = (f32[1,160,768]{2,1,0:T(8,128)S(1)}, f32[1,160,768]{2,1,0:T(8,128)}, u32[]{:S(2)}) copy-start(f32[1,160,768]{2,1,0:T(8,128)} %get-tuple-element.849) | copy-start | bytes 1474564
  1343.2 44.5 %copy-start.200 = (f32[1,160,768]{2,1,0:T(8,128)S(1)}, f32[1,160,768]{2,1,0:T(8,128)}, u32[]{:S(2)}) copy-start(f32[1,160,768]{2,1,0:T(8,128)} %get-tuple-element.848) | copy-start | bytes 1474564
  (197 other events, 660.8 us)
Sparse Core Ops, SparseCore 0:
  1190.5 55.4 reduce-scatter.32
  1249.8 54.5 reduce-scatter.30
  1306.8 62.5 reduce-scatter.14
  1375.9 98.9 reduce-scatter.28
  1480.6 98.1 reduce-scatter.26
  1583.5 61.9 reduce-scatter.18
  1649.8 65.2 reduce-scatter.24
  1719.7 89.0 reduce-scatter.16
  1814.0 110.8 reduce-scatter.22
  1929.5 111.1 reduce-scatter.20
where the time goes:
time: 2060 us; the launch traced here: 2050 us
  waiting for transfers between devices  1170 us (57%)
  local copies, waits for them, and re-layouts  308 us (15%)
  matrix products  250 us (12%)
  other arithmetic  192 us (9%)
  loops' own time  48.2 us (2%)
  blocking collectives  39.7 us (2%)
  starting transfers between devices  26.3 us (1%)
    ppermute x10, waiting for transfers between devices, from_behind(): lax.ppermute(value, axis, [(source, source + steps) for source in range(f...  526 us
    reduce_scatter x1, waiting for transfers between devices, per_device(): lax.psum_scatter(full_sum[3], 'dp', scatter_dimension=0, tiled=True)  116 us
    reduce_scatter x1, waiting for transfers between devices, per_device(): lax.psum_scatter(full_sum[2], 'dp', scatter_dimension=0, tiled=True)  116 us
    add x9, other arithmetic, settle(): running + addend  112 us
    reduce_scatter x1, waiting for transfers between devices, per_device(): lax.psum_scatter(cross_sum[0], ('section', 'dp'), scatter_dimension=1, ti...  104 us
    reduce_scatter x1, waiting for transfers between devices, per_device(): lax.psum_scatter(full_sum[0], 'dp', scatter_dimension=0, tiled=True)  93.7 us
    dot_general x20, matrix products, dense_left(): lax.dot_general(left, right, (((0,), (0,)), ((), ())), preferred_element_...  84.8 us
    reduce_scatter x1, waiting for transfers between devices, per_device(): lax.psum_scatter(cross_sum[1], ('section', 'dp'), scatter_dimension=1, ti...  76.8 us
  transfers between devices with their start and end apart: 20, of which 10 were waited for; matrix products, arithmetic and copies ran while one was open for 17% of the time, Pallas kernels for 0%

commit v1 on v0

v1 whole, which is shorter than its diff:
```python
import functools
import math

import jax
import jax.numpy as jnp
from jax import lax
from jax.experimental import pallas as pl
from jax.experimental.pallas import tpu as pltpu
from jax.sharding import PartitionSpec as P

HEADS = 12
EPSILON = 1e-06
MASKED = -1e30
BF = jnp.bfloat16
F32 = jnp.float32
PAD = 160
HALVES = 2
CHUNK = 32
LIMIT = 60 * 1024 * 1024
ANY = pl.BlockSpec(memory_space=pl.ANY)
SMEM = pl.BlockSpec(memory_space=pltpu.SMEM)
VMEM = pl.BlockSpec(memory_space=pltpu.VMEM)


def nn(left, right):
    return lax.dot_general(left, right, (((1,), (0,)), ((), ())), preferred_element_type=F32)


def nt(left, right):
    return lax.dot_general(left, right, (((1,), (1,)), ((), ())), preferred_element_type=F32)


def tn(left, right):
    return lax.dot_general(left, right, (((0,), (0,)), ((), ())), preferred_element_type=F32)


class Copies:
    def __init__(self, sems):
        self.sems, self.used, self.open = sems, 0, []

    def load(self, source, target):
        copy = pltpu.make_async_copy(source, target, self.sems.at[self.used])
        self.used += 1
        copy.start()
        return copy

    def store(self, source, target):
        self.open.append(self.load(source, target))

    def finish(self):
        for copy in self.open:
            copy.wait()


def by_rows(count, body):
    @pl.loop(0, count // CHUNK)
    def _(step):
        body(pl.ds(pl.multiple_of(step * CHUNK, CHUNK), CHUNK))


def standard(summed):
    centred = summed - jnp.mean(summed, -1, keepdims=True)
    inv_std = lax.rsqrt(jnp.mean(centred * centred, -1, keepdims=True) + EPSILON)
    return centred * inv_std, inv_std


def fold(value):
    return jnp.sum(value.reshape(value.shape[0] // 8, 8, value.shape[1]), 0)


def norm_back(grad_out, normed, inv_std, gain, sums, slot):
    sums[slot, 0] += fold(grad_out * normed)
    sums[slot, 1] += fold(grad_out)
    grad_normed = grad_out * gain
    return inv_std * (
        grad_normed
        - jnp.mean(grad_normed, -1, keepdims=True)
        - normed * jnp.mean(grad_normed * normed, -1, keepdims=True)
    )


def gelu_both(preact):
    size = jnp.abs(preact)
    bell = jnp.exp(-0.5 * preact * preact)
    t = 1.0 / (1.0 + (0.3275911 * math.sqrt(0.5)) * size)
    series = t * (
        0.5 * 0.254829592
        + t * (-0.5 * 0.284496736 + t * (0.5 * 1.421413741 + t * (-0.5 * 1.453152027 + t * (0.5 * 1.061405429))))
    )
    tail = series * bell
    below = jnp.where(preact >= 0.0, 1.0 - tail, tail)
    return preact * below, below + preact * bell * (1.0 / math.sqrt(2.0 * math.pi))


def head_lanes(width, head_dim):
    lane = lax.broadcasted_iota(jnp.int32, (1, width), 1)
    first = jnp.where(lane < head_dim, 1.0, 0.0)
    return first, 1.0 - first


def self_attend(qkv, mask, probs, att, groups, first_group, span, head_dim):
    width = 2 * head_dim
    model = att.shape[1]
    pairs = model // width
    low, high = head_lanes(width, head_dim)
    scale = 1.0 / math.sqrt(head_dim)
    low_b, high_b = (low * scale).astype(BF), (high * scale).astype(BF)

    @pl.loop(0, groups)
    def _(g):
        rows = pl.ds(pl.multiple_of(g * span, span), span)
        bias = mask[first_group + g]
        bias = jnp.concatenate([bias, bias], 0)
        for p in range(pairs):
            cols = p * width
            q = qkv[rows, cols : cols + width]
            k = qkv[rows, model + cols : model + cols + width]
            v = qkv[rows, 2 * model + cols : 2 * model + cols + width]
            both = jnp.concatenate([q * low_b, q * high_b], 0)
            scores = nt(both, k) + bias
            grown = jnp.exp(scores - jnp.max(scores, -1, keepdims=True))
            weights = (grown / jnp.sum(grown, -1, keepdims=True)).astype(BF)
            probs[g * pairs + p] = weights
            out = nn(weights, v)
            att[rows, cols : cols + width] = (out[:span] * low + out[span:] * high).astype(BF)


def self_attend_back(qkv, probs, grad_att, grad_qkv, groups, span, head_dim):
    width = 2 * head_dim
    model = grad_att.shape[1]
    pairs = model // width
    low, high = head_lanes(width, head_dim)
    scale = 1.0 / math.sqrt(head_dim)
    scaled = ((low * scale).astype(BF), (high * scale).astype(BF))
    plain = (low.astype(BF), high.astype(BF))

    @pl.loop(0, groups)
    def _(g):
        rows = pl.ds(pl.multiple_of(g * span, span), span)
        for p in range(pairs):
            cols = p * width
            q = qkv[rows, cols : cols + width]
            k = qkv[rows, model + cols : model + cols + width]
            v = qkv[rows, 2 * model + cols : 2 * model + cols + width]
            go = grad_att[rows, cols : cols + width]
            both_q = jnp.concatenate([q * scaled[0], q * scaled[1]], 0)
            both_g = jnp.concatenate([go * plain[0], go * plain[1]], 0)
            weights_b = probs[g * pairs + p]
            weights = weights_b.astype(F32)
            grad_w = nt(both_g, v)
            grad_s = (weights * (grad_w - jnp.sum(grad_w * weights, -1, keepdims=True))).astype(BF)
            out = nn(grad_s, k)
            grad_qkv[rows, cols : cols + width] = (
                out[:span] * (low * scale) + out[span:] * (high * scale)
            ).astype(BF)
            grad_qkv[rows, model + cols : model + cols + width] = tn(grad_s, both_q).astype(BF)
            grad_qkv[rows, 2 * model + cols : 2 * model + cols + width] = tn(weights_b, both_g).astype(BF)


def cross_attend(queries, keys, vals, image, first_row, probs, out, row_count, length, patches, head_dim):
    width = 2 * head_dim
    pairs = queries.shape[1] // width
    low, high = head_lanes(width, head_dim)
    scale = 1.0 / math.sqrt(head_dim)
    low_s, high_s = low * scale, high * scale
    shown = lax.broadcasted_iota(jnp.int32, (2 * length, keys.shape[1]), 1) < patches

    @pl.loop(0, row_count)
    def _(r):
        rows = pl.ds(pl.multiple_of(r * length, 8), length)
        picked = image[first_row + r]
        for p in range(pairs):
            cols = slice(p * width, p * width + width)
            q = queries[rows, cols]
            both = jnp.concatenate([q * low_s, q * high_s], 0).astype(BF)
            scores = jnp.where(shown, nt(both, keys[picked, :, cols]), MASKED)
            grown = jnp.exp(scores - jnp.max(scores, -1, keepdims=True))
            weights = (grown / jnp.sum(grown, -1, keepdims=True)).astype(BF)
            probs[r * pairs + p] = weights
            got = nn(weights, vals[picked, :, cols])
            out[rows, cols] = got[:length] * low + got[length:] * high


def cross_attend_back(
    queries, keys, vals, image, first_row, probs, grad_att, grad_q, grad_k, grad_v, row_count, length, head_dim
):
    width = 2 * head_dim
    pairs = queries.shape[1] // width
    low, high = head_lanes(width, head_dim)
    scale = 1.0 / math.sqrt(head_dim)
    low_s, high_s = low * scale, high * scale

    @pl.loop(0, row_count)
    def _(r):
        rows = pl.ds(pl.multiple_of(r * length, 8), length)
        picked = image[first_row + r]
        for p in range(pairs):
            cols = slice(p * width, p * width + width)
            q = queries[rows, cols]
            go = grad_att[rows, cols]
            both_q = jnp.concatenate([q * low_s, q * high_s], 0).astype(BF)
            both_g = jnp.concatenate([go * low, go * high], 0).astype(BF)
            weights_b = probs[r * pairs + p]
            weights = weights_b.astype(F32)
            grad_w = nt(both_g, vals[picked, :, cols])
            grad_s = (weights * (grad_w - jnp.sum(grad_w * weights, -1, keepdims=True))).astype(BF)
            got = nn(grad_s, keys[picked, :, cols])
            grad_q[rows, cols] = got[:length] * low_s + got[length:] * high_s
            grad_k[picked, :, cols] = tn(grad_s, both_q).astype(BF)
            grad_v[picked, :, cols] = tn(weights_b, both_g).astype(BF)


def grow(entry, w_up, preact, hidden, slope):
    tile = preact.shape[1]
    for j in range(hidden.shape[1] // tile):
        cols = slice(j * tile, j * tile + tile)
        preact[...] = nn(entry[...], w_up[:, cols])

        def body(rows):
            value, rise = gelu_both(preact[rows, :])
            hidden[rows, cols] = value.astype(BF)
            slope[rows, cols] = rise.astype(BF)

        by_rows(preact.shape[0], body)


def shrink(branch, w_down, slope, grad_pre):
    tile = branch.shape[1]
    for j in range(slope.shape[1] // tile):
        cols = slice(j * tile, j * tile + tile)
        grad_pre[:, cols] = (nt(branch[...], w_down[cols, :]) * slope[:, cols].astype(F32)).astype(BF)


def text_forward_kernel(half, span, flag, gains, biases, mask, text, wqkv, wo, w1, w2, *refs):
    (lay, zb, hidden, att), refs = refs[4:8] if half else refs[:4], refs[8:] if half else refs[4:]
    (bnd, y1, y3, qkv, probs, slope), refs = refs[:6], refs[6:]
    (x_s, wqkv_s, wo_s, w1_s, w2_s, qkv_s, probs_s, att_s, y1_s, mid_s, zb_s, pre_s, hid_s, slo_s, y3_s, out_s, sems) = refs
    count = x_s.shape[0]
    own = pl.ds(half * count, count)

    @pl.when(flag[0] == 0)
    def _():
        cp = Copies(sems)
        gets = [cp.load(text.at[own], x_s)] + [
            cp.load(a, b) for a, b in ((wqkv, wqkv_s), (wo, wo_s), (w1, w1_s), (w2, w2_s))
        ]
        gets[0].wait()
        gets[1].wait()
        qkv_s[...] = nn(x_s[...], wqkv_s[...]).astype(BF)
        cp.store(qkv_s, qkv)
        groups = count // span
        self_attend(qkv_s, mask, probs_s, att_s, groups, half * groups, span, x_s.shape[1] // HEADS)
        cp.store(probs_s, probs)
        cp.store(att_s, att.at[own])
        gets[2].wait()
        y1_s[...] = x_s[...].astype(F32) + nn(att_s[...], wo_s[...])
        cp.store(y1_s, y1)

        def first(rows):
            value = standard(y1_s[rows, :])[0] * gains[0:1, :] + biases[0:1, :]
            mid_s[rows, :] = value
            zb_s[rows, :] = value.astype(BF)

        by_rows(count, first)
        cp.store(zb_s, zb.at[own])
        gets[3].wait()
        grow(zb_s, w1_s, pre_s, hid_s, slo_s)
        cp.store(hid_s, hidden.at[own])
        cp.store(slo_s, slope)
        gets[4].wait()
        y3_s[...] = mid_s[...] + nn(hid_s[...], w2_s[...])
        cp.store(y3_s, y3)

        def second(rows):
            out_s[rows, :] = (standard(y3_s[rows, :])[0] * gains[1:2, :] + biases[1:2, :]).astype(BF)

        by_rows(count, second)
        cp.store(out_s, bnd)
        cp.store(out_s, lay.at[own])
        cp.finish()


def text_ffn_back_kernel(half, flag, gains, grad, y3, slope, w1, w2, *refs):
    (df, du, sums), refs = refs[3:6], refs[6:]
    dmid, refs = refs[0], refs[1:]
    (g_s, y3_s, slo_s, w1_s, w2_s, dy_s, df_s, du_s, dm_s, sum_s, sems) = refs
    count = g_s.shape[0]
    own = pl.ds(half * count, count)

    @pl.when(flag[0] == 0)
    def _():
        cp = Copies(sems)
        gets = [
            cp.load(a, b) for a, b in ((grad, g_s), (y3, y3_s), (w2, w2_s), (slope, slo_s), (w1, w1_s))
        ]
        sum_s[...] = jnp.zeros_like(sum_s)
        gets[0].wait()
        gets[1].wait()

        def body(rows):
            normed, inv_std = standard(y3_s[rows, :])
            value = norm_back(g_s[rows, :].astype(F32), normed, inv_std, gains[1:2, :], sum_s, 0)
            dy_s[rows, :] = value
            df_s[rows, :] = value.astype(BF)

        by_rows(count, body)
        cp.store(df_s, df.at[own])
        cp.store(sum_s, sums.at[half, pl.ds(1, 1)])
        gets[2].wait()
        gets[3].wait()
        shrink(df_s, w2_s, slo_s, du_s)
        cp.store(du_s, du.at[own])
        gets[4].wait()
        dm_s[...] = dy_s[...] + nt(du_s[...], w1_s[...])
        cp.store(dm_s, dmid)
        cp.finish()


def text_self_back_kernel(half, span, flag, gains, dmid, y1, qkv, probs, wo, wqkv, *refs):
    (da, dqkv, ig, sums), refs = refs[4:8], refs[8:]
    (dm_s, y1_s, qkv_s, probs_s, wo_s, wqkv_s, dy_s, da_s, datt_s, dqkv_s, ig_s, sum_s, sems) = refs
    count = dm_s.shape[0]
    own = pl.ds(half * count, count)

    @pl.when(flag[0] == 0)
    def _():
        cp = Copies(sems)
        gets = [
            cp.load(a, b)
            for a, b in ((dmid, dm_s), (y1, y1_s), (wo, wo_s), (qkv, qkv_s), (probs, probs_s), (wqkv, wqkv_s))
        ]
        sum_s[...] = jnp.zeros_like(sum_s)
        gets[0].wait()
        gets[1].wait()

        def body(rows):
            normed, inv_std = standard(y1_s[rows, :])
            value = norm_back(dm_s[rows, :], normed, inv_std, gains[0:1, :], sum_s, 0)
            dy_s[rows, :] = value
            da_s[rows, :] = value.astype(BF)

        by_rows(count, body)
        cp.store(da_s, da.at[own])
        cp.store(sum_s, sums.at[half, pl.ds(0, 1)])
        gets[2].wait()
        datt_s[...] = nt(da_s[...], wo_s[...]).astype(BF)
        gets[3].wait()
        gets[4].wait()
        self_attend_back(qkv_s, probs_s, datt_s, dqkv_s, count // span, span, dm_s.shape[1] // HEADS)
        cp.store(dqkv_s, dqkv.at[own])
        gets[5].wait()
        ig_s[...] = dy_s[...] + nt(dqkv_s[...], wqkv_s[...])
        cp.store(ig_s, ig.at[own])
        cp.finish()


JOIN_BUFS = 16


def joining_kernel(half, span, length, patches, flag, image, gains, biases, cgain, cbias, mask, bnd, cot,
                   wqkv, wo, w1, w2, wq, wc, keys, vals, *refs):
    refs = refs[JOIN_BUFS:] if half else refs[4:]
    (lay, zb, hidden, att, ig, df, du, da, dqkv, sums, midb, dq, catt, dca, dkey, dval), refs = refs[:16], refs[16:]
    back, refs = refs[0], refs[1:]
    (x_s, wqkv_s, wo_s, w1_s, w2_s, wq_s, wc_s, key_s, val_s, cot_s, qkv_s, probs_s, att_s, y1_s, mid_s, midb_s,
     qc_s, cprobs_s, cat_s, catb_s, y2_s, zb_s, pre_s, hid_s, slo_s, y3_s, lay_s, df_s, dy_s, du_s, dz_s, dca_s,
     dkey_s, dval_s, dqb_s, da_s, datt_s, dqkv_s, sum_s, sems) = refs
    count, model = x_s.shape
    head_dim = model // HEADS
    own = pl.ds(half * count, count)
    row_count = count // length
    groups = count // span
    pictures = pl.ds(half * row_count, row_count)

    @pl.when(flag[0] == 1)
    def _():
        cp = Copies(sems)
        (g_x, g_qkv, g_o, g_q, g_key, g_val, g_c, g_1, g_2, g_cot) = [
            cp.load(a, b)
            for a, b in (
                (bnd, x_s), (wqkv, wqkv_s), (wo, wo_s), (wq, wq_s), (keys.at[pictures], key_s),
                (vals.at[pictures], val_s), (wc, wc_s), (w1, w1_s), (w2, w2_s), (cot.at[own], cot_s),
            )
        ]
        sum_s[...] = jnp.zeros_like(sum_s)
        g_x.wait()
        g_qkv.wait()
        qkv_s[...] = nn(x_s[...], wqkv_s[...]).astype(BF)
        self_attend(qkv_s, mask, probs_s, att_s, groups, half * groups, span, head_dim)
        cp.store(att_s, att.at[own])
        g_o.wait()
        y1_s[...] = x_s[...].astype(F32) + nn(att_s[...], wo_s[...])

        def first(rows):
            value = standard(y1_s[rows, :])[0] * gains[0:1, :] + biases[0:1, :]
            mid_s[rows, :] = value
            midb_s[rows, :] = value.astype(BF)

        by_rows(count, first)
        cp.store(midb_s, midb.at[own])
        g_q.wait()
        qc_s[...] = nn(midb_s[...], wq_s[...]).astype(BF).astype(F32)
        g_key.wait()
        g_val.wait()
        cross_attend(qc_s, key_s, val_s, image, half * row_count, cprobs_s, cat_s, row_count, length, patches, head_dim)
        catb_s[...] = cat_s[...].astype(BF)
        cp.store(catb_s, catt.at[own])
        g_c.wait()
        y2_s[...] = mid_s[...] + nn(catb_s[...], wc_s[...])

        def second(rows):
            value = standard(y2_s[rows, :])[0] * cgain[...] + cbias[...]
            mid_s[rows, :] = value
            zb_s[rows, :] = value.astype(BF)

        by_rows(count, second)
        cp.store(zb_s, zb.at[own])
        g_1.wait()
        grow(zb_s, w1_s, pre_s, hid_s, slo_s)
        cp.store(hid_s, hidden.at[own])
        g_2.wait()
        y3_s[...] = mid_s[...] + nn(hid_s[...], w2_s[...])
        g_cot.wait()

        def third(rows):
            normed, inv_std = standard(y3_s[rows, :])
            lay_s[rows, :] = (normed * gains[1:2, :] + biases[1:2, :]).astype(BF)
            value = norm_back(cot_s[rows, :].astype(F32), normed, inv_std, gains[1:2, :], sum_s, 1)
            dy_s[rows, :] = value
            df_s[rows, :] = value.astype(BF)

        by_rows(count, third)
        cp.store(lay_s, lay.at[own])
        cp.store(df_s, df.at[own])
        shrink(df_s, w2_s, slo_s, du_s)
        cp.store(du_s, du.at[own])
        dz_s[...] = dy_s[...] + nt(du_s[...], w1_s[...])

        def fourth(rows):
            normed, inv_std = standard(y2_s[rows, :])
            value = norm_back(dz_s[rows, :], normed, inv_std, cgain[...], sum_s, 2)
            dy_s[rows, :] = value
            dca_s[rows, :] = value.astype(BF)

        by_rows(count, fourth)
        cp.store(dca_s, dca.at[own])
        cat_s[...] = nt(dca_s[...], wc_s[...]).astype(BF).astype(F32)
        cross_attend_back(qc_s, key_s, val_s, image, half * row_count, cprobs_s, cat_s, pre_s, dkey_s, dval_s,
                          row_count, length, head_dim)
        cp.store(dkey_s, dkey.at[pictures])
        cp.store(dval_s, dval.at[pictures])
        dqb_s[...] = pre_s[...].astype(BF)
        cp.store(dqb_s, dq.at[own])
        dz_s[...] = dy_s[...] + nt(dqb_s[...], wq_s[...])

        def fifth(rows):
            normed, inv_std = standard(y1_s[rows, :])
            value = norm_back(dz_s[rows, :], normed, inv_std, gains[0:1, :], sum_s, 0)
            dy_s[rows, :] = value
            da_s[rows, :] = value.astype(BF)

        by_rows(count, fifth)
        cp.store(da_s, da.at[own])
        cp.store(sum_s, sums.at[half])
        datt_s[...] = nt(da_s[...], wo_s[...]).astype(BF)
        self_attend_back(qkv_s, probs_s, datt_s, dqkv_s, groups, span, head_dim)
        cp.store(dqkv_s, dqkv.at[own])
        dz_s[...] = dy_s[...] + nt(dqkv_s[...], wqkv_s[...])
        x_s[...] = dz_s[...].astype(BF)
        cp.store(x_s, back)
        cp.store(dz_s, ig.at[own])
        cp.finish()


def project_kernel(flag, image, weight, out, packed):
    @pl.when(flag[0] == 1)
    def _():
        each, patches = image.shape[0], image.shape[1]
        packed[...] = jnp.zeros_like(packed)
        for i in range(each):
            packed[i * PAD : i * PAD + patches, :] = image[i]
        got = nn(packed[...], weight[...]).astype(BF)
        for i in range(each):
            out[i] = got[i * PAD : i * PAD + PAD]


def image_back_kernel(flag, image, dkey, dval, wk, wv, own, other, dwk, dwv, packed, sum_k, sum_v):
    step = pl.program_id(0)

    @pl.when(flag[0] == 1)
    def _():
        each, patches, width = image.shape

        @pl.when(step == 0)
        def _():
            packed[...] = jnp.zeros_like(packed)
            sum_k[...] = jnp.zeros_like(sum_k)
            sum_v[...] = jnp.zeros_like(sum_v)

        for i in range(each):
            packed[i * PAD : i * PAD + patches, :] = image[i]
        grad_k = dkey[...].reshape(each * PAD, dkey.shape[2])
        grad_v = dval[...].reshape(each * PAD, dval.shape[2])
        sum_k[...] += tn(packed[...], grad_k)
        sum_v[...] += tn(packed[...], grad_v)
        part = width // 2
        got = nt(grad_k, wk[part:, :]) + nt(grad_v, wv[part:, :])
        for i in range(each):
            own[i] = got[i * PAD : i * PAD + patches]
        got = (nt(grad_k, wk[:part, :]) + nt(grad_v, wv[:part, :])).astype(BF)
        for i in range(each):
            other[i] = got[i * PAD : i * PAD + patches]

        @pl.when(step == pl.num_programs(0) - 1)
        def _():
            dwk[...] = sum_k[...].astype(BF)
            dwv[...] = sum_v[...].astype(BF)


def weight_grad_kernel(left, right, out):
    out[...] = tn(left[...], right[...]).astype(BF)


def weight_grad(left, right, by_left, tile=768):
    tokens, rows = left.shape
    cols = right.shape[1]
    if by_left:
        grid, specs = (rows // tile,), (lambda i: (0, i), lambda i: (0, 0), lambda i: (i, 0))
        shapes = ((tokens, tile), (tokens, cols), (tile, cols))
    else:
        grid, specs = (cols // tile,), (lambda i: (0, 0), lambda i: (0, i), lambda i: (0, i))
        shapes = ((tokens, rows), (tokens, tile), (rows, tile))
    return pl.pallas_call(
        weight_grad_kernel,
        grid=grid,
        in_specs=[pl.BlockSpec(shapes[0], specs[0]), pl.BlockSpec(shapes[1], specs[1])],
        out_specs=pl.BlockSpec(shapes[2], specs[2]),
        out_shape=jax.ShapeDtypeStruct((rows, cols), BF),
        compiler_params=pltpu.CompilerParams(vmem_limit_bytes=LIMIT),
        cost_estimate=pl.CostEstimate(
            flops=2 * tokens * rows * cols, bytes_accessed=2 * (tokens * (rows + cols) + rows * cols), transcendentals=0
        ),
        name="weight_grad",
    )(left, right)


def stage(kernel, name, smem, vmem, hbm, bufs, fresh, scratch, flops):
    arrays = [b for b in bufs if not isinstance(b, jax.ShapeDtypeStruct)]
    first = len(smem) + len(vmem) + len(hbm)
    aliases, at = {}, first
    for i, b in enumerate(bufs):
        if not isinstance(b, jax.ShapeDtypeStruct):
            aliases[at] = i
            at += 1
    outs = [jax.ShapeDtypeStruct(b.shape, b.dtype) for b in list(bufs) + list(fresh)]
    got = pl.pallas_call(
        kernel,
        in_specs=[SMEM] * len(smem) + [VMEM] * len(vmem) + [ANY] * (len(hbm) + len(arrays)),
        out_specs=[ANY] * len(outs),
        out_shape=outs,
        scratch_shapes=list(scratch) + [pltpu.SemaphoreType.DMA((40,))],
        input_output_aliases=aliases,
        compiler_params=pltpu.CompilerParams(vmem_limit_bytes=LIMIT),
        cost_estimate=pl.CostEstimate(flops=flops, bytes_accessed=sum(a.size * 2 for a in hbm), transcendentals=0),
        name=name,
    )(*smem, *vmem, *hbm, *arrays)
    return list(got[: len(bufs)]), list(got[len(bufs) :])


def spread(value, axis_size):
    return value.reshape(axis_size, value.shape[0] // axis_size, value.shape[1])


def reduce_parts(value, only):
    total = lax.axis_size("dp")
    if total != 16:
        return lax.psum_scatter(value, "dp", scatter_dimension=0, tiled=True)[0].astype(F32)
    place = lax.axis_index("dp")
    core, y, z = place % 2, (place // 2) % 2, place // 4
    rows, cols = value.shape[1:]

    def swap(sent, flip):
        perm = [(s * total + i, s * total + (i ^ flip)) for s in only for i in range(total)]
        return lax.ppermute(sent, ("section", "dp"), perm)

    def pick(array, axis, index):
        return lax.dynamic_index_in_dim(array, index, axis, keepdims=False)

    value = value.reshape(8, 2, rows, cols)
    got = swap(pick(value, 1, 1 - core), 1)
    value = (pick(value, 1, core).astype(F32) + got.astype(F32)).astype(BF)
    value = value.reshape(4, 2, rows, cols)
    got = swap(pick(value, 1, 1 - y), 2)
    value = (pick(value, 1, y).astype(F32) + got.astype(F32)).astype(BF)
    others = [swap(pick(value, 0, z ^ step), 4 * step) for step in (1, 2, 3)]
    return pick(value, 0, z).astype(F32) + others[0].astype(F32) + others[1].astype(F32) + others[2].astype(F32)


def per_device(
    text_in, cotangent, images, segment_ids, row_image, self_qkv, self_out, ffn_up, ffn_down,
    norm_gain, norm_bias, image_kv, cross_query, cross_out, cross_gain, cross_bias,
):
    tokens, model = text_in.shape
    row_total, length = segment_ids.shape
    patches, width = images.shape[1:]
    hidden_width = ffn_up.shape[2]
    block_rows = row_image.shape[1]
    head_dim = model // HEADS
    pairs = HEADS // 2
    count = tokens // HALVES
    half_rows = row_total // HALVES
    span = 2 * length
    dp = lax.axis_size("dp")
    section = lax.axis_index("section")
    is_text = section == 0
    flag = section.astype(jnp.int32).reshape(1)
    place = lax.axis_index("dp")
    wqkv, wo, w1, w2 = self_qkv[0], self_out[0], ffn_up[0], ffn_down[0]
    gains, biases = norm_gain[0], norm_bias[0]
    cgain, cbias = cross_gain.reshape(1, model), cross_bias.reshape(1, model)

    marks = (segment_ids + segment_ids.shape[1] * (jnp.arange(row_total, dtype=jnp.int32) % 2)[:, None]).reshape(-1, span)
    mask = jnp.where(marks[:, :, None] == marks[:, None, :], 0.0, MASKED).astype(F32)
    in_block = jnp.arange(row_total, dtype=jnp.int32) // block_rows * block_rows % half_rows
    image = row_image.reshape(-1) + in_block

    def shape(*dims, dtype=BF):
        return jax.ShapeDtypeStruct(dims, dtype)

    core = place % 2
    half_w = width // 2
    sent_w = lax.dynamic_slice_in_dim(image_kv, core * half_w, half_w, 0)
    sent_w = lax.ppermute(sent_w, "section", [(0, 1)])
    swapped = lax.ppermute(sent_w, "dp", [(i, i ^ 1) for i in range(dp)])
    key_w = jnp.where(core == 0, jnp.concatenate([sent_w, swapped], 0), jnp.concatenate([swapped, sent_w], 0))

    each = 4
    grid = row_total // each

    def project(weight):
        return pl.pallas_call(
            project_kernel,
            grid_spec=pltpu.PrefetchScalarGridSpec(
                num_scalar_prefetch=1,
                grid=(grid,),
                in_specs=[
                    pl.BlockSpec((each, patches, width), lambda i, f: (i * f[0], 0, 0)),
                    pl.BlockSpec((width, model), lambda i, f: (0, 0)),
                ],
                out_specs=pl.BlockSpec((each, PAD, model), lambda i, f: (i * f[0], 0, 0)),
                scratch_shapes=[pltpu.VMEM((each * PAD, width), BF)],
            ),
            out_shape=shape(row_total, PAD, model),
            compiler_params=pltpu.CompilerParams(vmem_limit_bytes=LIMIT),
            cost_estimate=pl.CostEstimate(
                flops=2 * row_total * PAD * width * model, bytes_accessed=12_000_000, transcendentals=0
            ),
            name="project",
        )(flag, images, weight)

    vm = pltpu.VMEM
    probs_shape = (count // span * pairs, 2 * span, span)
    text_scratch = [
        vm((count, model), BF), vm(wqkv.shape, BF), vm(wo.shape, BF), vm(w1.shape, BF), vm(w2.shape, BF),
        vm((count, 3 * model), BF), vm(probs_shape, BF), vm((count, model), BF), vm((count, model), F32),
        vm((count, model), F32), vm((count, model), BF), vm((count, model), F32), vm((count, hidden_width), BF),
        vm((count, hidden_width), BF), vm((count, model), F32), vm((count, model), BF),
    ]
    shared = [shape(tokens, model), shape(tokens, model), shape(tokens, hidden_width), shape(tokens, model)]
    linear = model * 3 * model + model * model + 2 * model * hidden_width
    kept, outward = [], []
    for half in range(HALVES):
        shared, fresh = stage(
            functools.partial(text_forward_kernel, half, span), "text_forward", [flag], [gains, biases, mask],
            [text_in, wqkv, wo, w1, w2], shared,
            [
                shape(count, model), shape(count, model, dtype=F32), shape(count, model, dtype=F32),
                shape(count, 3 * model), shape(*probs_shape), shape(count, hidden_width),
            ],
            text_scratch, 2 * count * linear,
        )
        outward.append(lax.ppermute(fresh[0], "section", [(0, 1)]))
        kept.append(fresh[1:])
    values = project(image_kv)
    keys = project(key_w)

    join_scratch = [
        vm((count, model), BF), vm(wqkv.shape, BF), vm(wo.shape, BF), vm(w1.shape, BF), vm(w2.shape, BF),
        vm(cross_query.shape, BF), vm(cross_out.shape, BF), vm((half_rows, PAD, model), BF),
        vm((half_rows, PAD, model), BF), vm((count, model), BF), vm((count, 3 * model), BF), vm(probs_shape, BF),
        vm((count, model), BF), vm((count, model), F32), vm((count, model), F32), vm((count, model), BF),
        vm((count, model), F32), vm((half_rows * pairs, 2 * length, PAD), BF), vm((count, model), F32),
        vm((count, model), BF), vm((count, model), F32), vm((count, model), BF), vm((count, model), F32),
        vm((count, hidden_width), BF), vm((count, hidden_width), BF), vm((count, model), F32), vm((count, model), BF),
        vm((count, model), BF), vm((count, model), F32), vm((count, hidden_width), BF), vm((count, model), F32),
        vm((count, model), BF), vm((half_rows, PAD, model), BF), vm((half_rows, PAD, model), BF),
        vm((count, model), BF), vm((count, model), BF), vm((count, model), BF), vm((count, 3 * model), BF),
        vm((3, 2, 8, model), F32),
    ]
    bufs = shared + [
        shape(tokens, model, dtype=F32), shape(tokens, model), shape(tokens, hidden_width), shape(tokens, model),
        shape(tokens, 3 * model), shape(HALVES, 3, 2, 8, model, dtype=F32), shape(tokens, model), shape(tokens, model),
        shape(tokens, model), shape(tokens, model), shape(row_total, PAD, model), shape(row_total, PAD, model),
    ]
    returned = []
    for half in range(HALVES):
        bufs, fresh = stage(
            functools.partial(joining_kernel, half, span, length, patches), "joining", [flag, image],
            [gains, biases, cgain, cbias, mask],
            [outward[half], cotangent, wqkv, wo, w1, w2, cross_query, cross_out, keys, values],
            bufs, [shape(count, model)], join_scratch, 4 * count * (linear + 2 * model * model),
        )
        returned.append(lax.ppermute(fresh[0], "section", [(1, 0)]))
    lay, zb, hidden, att, ig, df, du, da, dqkv, sums, midb, dq, catt, dca, dkey, dval = bufs

    own_part, other_part, grad_wk, grad_wv = pl.pallas_call(
        image_back_kernel,
        grid_spec=pltpu.PrefetchScalarGridSpec(
            num_scalar_prefetch=1,
            grid=(grid,),
            in_specs=[
                pl.BlockSpec((each, patches, width), lambda i, f: (i * f[0], 0, 0)),
                pl.BlockSpec((each, PAD, model), lambda i, f: (i * f[0], 0, 0)),
                pl.BlockSpec((each, PAD, model), lambda i, f: (i * f[0], 0, 0)),
                pl.BlockSpec((width, model), lambda i, f: (0, 0)),
                pl.BlockSpec((width, model), lambda i, f: (0, 0)),
            ],
            out_specs=[
                pl.BlockSpec((each, patches, width // 2), lambda i, f: (i * f[0], 0, 0)),
                pl.BlockSpec((each, patches, width // 2), lambda i, f: (i * f[0], 0, 0)),
                pl.BlockSpec((width, model), lambda i, f: (0, 0)),
                pl.BlockSpec((width, model), lambda i, f: (0, 0)),
            ],
            scratch_shapes=[vm((each * PAD, width), BF), vm((width, model), F32), vm((width, model), F32)],
        ),
        out_shape=[
            shape(row_total, patches, width // 2, dtype=F32), shape(row_total, patches, width // 2),
            shape(width, model), shape(width, model),
        ],
        compiler_params=pltpu.CompilerParams(vmem_limit_bytes=LIMIT),
        cost_estimate=pl.CostEstimate(
            flops=8 * row_total * PAD * width * model, bytes_accessed=25_000_000, transcendentals=0
        ),
        name="image_back",
    )(flag, images, dkey, dval, key_w, image_kv)
    image_part = lax.ppermute(other_part, "section", [(1, 0)])

    grad_cq = weight_grad(dq, midb, True)
    grad_co = weight_grad(dca, catt, True)
    sections = lax.axis_size("section")
    cross_rows = model // (sections * dp)

    def by_owner(value):
        value = value.reshape(sections, dp, cross_rows, model)
        return jnp.swapaxes(value, 0, 1).reshape(dp, sections * cross_rows, model)

    joint = jnp.concatenate(
        [spread(grad_wk, dp), spread(grad_wv, dp), by_owner(grad_cq), by_owner(grad_co)], 1
    )
    joint = reduce_parts(joint, (1,))
    image_rows = width // dp

    dmids = []
    for half in range(HALVES):
        y1, y3, qkv, probs, slope = kept[half]
        (df, du, sums), fresh = stage(
            functools.partial(text_ffn_back_kernel, half), "text_ffn_back", [flag], [gains],
            [returned[half], y3, slope, w1, w2], [df, du, sums], [shape(count, model, dtype=F32)],
            [
                vm((count, model), BF), vm((count, model), F32), vm((count, hidden_width), BF), vm(w1.shape, BF),
                vm(w2.shape, BF), vm((count, model), F32), vm((count, model), BF), vm((count, hidden_width), BF),
                vm((count, model), F32), vm((1, 2, 8, model), F32),
            ],
            4 * count * model * hidden_width,
        )
        dmids.append(fresh[0])
    down = reduce_parts(spread(weight_grad(hidden, df, True), dp), (0, 1))
    up = reduce_parts(spread(weight_grad(zb, du, False), dp), (0, 1))
    for half in range(HALVES):
        y1, y3, qkv, probs, slope = kept[half]
        (da, dqkv, ig, sums), _ = stage(
            functools.partial(text_self_back_kernel, half, span), "text_self_back", [flag], [gains],
            [dmids[half], y1, qkv, probs, wo, wqkv], [da, dqkv, ig, sums], [],
            [
                vm((count, model), F32), vm((count, model), F32), vm((count, 3 * model), BF), vm(probs_shape, BF),
                vm(wo.shape, BF), vm(wqkv.shape, BF), vm((count, model), F32), vm((count, model), BF),
                vm((count, model), BF), vm((count, 3 * model), BF), vm((count, model), F32), vm((1, 2, 8, model), F32),
            ],
            2 * count * 4 * model * model,
        )
    entry = jnp.where(is_text, text_in, jnp.concatenate(outward, 0))
    qkv_grad = reduce_parts(spread(weight_grad(entry, dqkv, False), dp), (0, 1))

    totals = jnp.sum(sums, (0, 3))
    own_norm = totals[:2].reshape(4, dp, model // dp)
    own_cross = jnp.where(is_text, 0.0, totals[2]).reshape(2, sections, dp, cross_rows)
    small = jnp.concatenate(
        [jnp.moveaxis(own_norm, 1, 0).reshape(dp, -1), jnp.moveaxis(own_cross, 2, 0).reshape(dp, -1)], 1
    )
    small = jnp.pad(small[:, None, :], ((0, 0), (0, 15), (0, model - small.shape[1]))).astype(BF)
    last = reduce_parts(jnp.concatenate([spread(weight_grad(att, da, True), dp), small], 1), (0, 1))
    out_rows = model // dp
    out_grad, small = last[:out_rows], last[out_rows]
    norm_part = small[: 4 * out_rows].reshape(2, 2, out_rows)
    cross_part = small[4 * out_rows : 4 * out_rows + 2 * sections * cross_rows].reshape(2, sections, cross_rows)

    at = 2 * image_rows
    cross_q = joint[at : at + sections * cross_rows]
    cross_o = joint[at + sections * cross_rows :]
    extra = jnp.pad(cross_part[:, 0].reshape(1, -1), ((0, 15), (0, model - 2 * cross_rows)))
    parcel = jnp.concatenate([joint[:image_rows], cross_q[:cross_rows], cross_o[:cross_rows], extra], 0).astype(BF)
    parcel = lax.ppermute(parcel, "section", [(1, 0)]).astype(F32)
    at = image_rows + 2 * cross_rows
    pick = functools.partial(jnp.where, is_text)
    grad_kv = pick(parcel[:image_rows], joint[image_rows : 2 * image_rows])
    grad_cross_q = pick(parcel[image_rows : image_rows + cross_rows], cross_q[cross_rows:]).T
    grad_cross_o = pick(parcel[image_rows + cross_rows : at], cross_o[cross_rows:]).T
    grad_cross_g = pick(parcel[at, :cross_rows], cross_part[0, 1])
    grad_cross_b = pick(parcel[at, cross_rows : 2 * cross_rows], cross_part[1, 1])
    image_grad = pick(image_part.astype(F32), own_part)
    return (
        lay[None], ig[None], image_grad, qkv_grad[None], out_grad[None], up[None], down[None],
        norm_part[:, 0][None], norm_part[:, 1][None], grad_kv, grad_cross_q, grad_cross_o, grad_cross_g, grad_cross_b,
    )


def solution(mesh):
    return jax.shard_map(
        per_device,
        mesh=mesh,
        in_specs=(
            P("dp", None),
            P("dp", None),
            P("dp", None, None),
            P("dp", None),
            P("dp", None),
            P("section", None, None),
            P("section", None, None),
            P("section", None, None),
            P("section", None, None),
            P("section", None, None),
            P("section", None, None),
            P(None, "section"),
            P(),
            P(),
            P(),
            P(),
        ),
        out_specs=(
            P("section", "dp", None),
            P("section", "dp", None),
            P("dp", None, "section"),
            P("section", "dp", None),
            P("section", "dp", None),
            P("section", "dp", None),
            P("section", "dp", None),
            P("section", None, "dp"),
            P("section", None, "dp"),
            P("dp", "section"),
            P(None, ("section", "dp")),
            P(None, ("section", "dp")),
            P(("section", "dp")),
            P(("section", "dp")),
        ),
        check_vma=False,
    )
```

time: 2060 us -> 540 us (0.26)
  the two profiles are of different devices: /device:TPU:0 before, /device:TPU:16 now
where the time goes in v1:
time: 540 us; the launch traced here: 530 us
  waiting for transfers between devices  260 us (48%)
  Pallas kernels  161 us (30%)
  local copies, waits for them, and re-layouts  41.6 us (8%)
  starting transfers between devices  36.2 us (7%)
  other arithmetic  28.8 us (5%)
    ppermute x2, waiting for transfers between devices, per_device(): returned.append(lax.ppermute(fresh[0], 'section', [(1, 0)]))  149 us
    pallas_call x8, Pallas kernels, stage(): pl.pallas_call(kernel, in_specs=[SMEM] * len(smem) + [VMEM] * len(vmem) +...  117 us
    ppermute x25, waiting for transfers between devices, swap(): return lax.ppermute(sent, ('section', 'dp'), perm)  89.7 us
    pallas_call x6, Pallas kernels, weight_grad(): pl.pallas_call(weight_grad_kernel, grid=grid, in_specs=[pl.BlockSpec(shap...  33 us
    ppermute x25, starting transfers between devices, swap(): return lax.ppermute(sent, ('section', 'dp'), perm)  24.9 us
    ppermute x1, waiting for transfers between devices, per_device(): parcel = lax.ppermute(parcel, 'section', [(1, 0)]).astype(F32)  21.7 us
    unnamed x41, local copies, waits for them, and re-layouts  17.8 us
    squeeze x15, local copies, waits for them, and re-layouts, pick(): return lax.dynamic_index_in_dim(array, index, axis, keepdims=False)  12.4 us
  transfers between devices with their start and end apart: 33, of which 14 were waited for; matrix products, arithmetic and copies ran while one was open for 11% of the time, Pallas kernels for 25%

profile of v1, /device:TPU:16, one launch (start us, length us, event | category | flops | bytes accessed | tf_op | source)
XLA Modules:
  0.0 529.9 jit_solution(602606126429995462)
XLA Ops:
  1.9 3.4 collective-permute-start.1
  7.0 22.2 %text_forward.2 = (bf16[640,768]{1,0:T(8,128)(2,1)}, bf16[640,768]{1,0:T(8,128)(2,1)}, bf16[640,3072]{1,0:T(8,128)(2,1)}, bf16[640,768]{1,0:T(8,128)(2,1)}, bf16...) custom-call(s32[1]{0:T(128)} %bitcast.flag, ...), custom_call_target="tpu_custom_call" | custom-call | flops 4529848320 | bytes 15138816 | tf_op jit(solution)/shard_map/text_forward/pallas_call | solution.py:556
  30.6 22.5 %text_forward.3 = (bf16[640,768]{1,0:T(8,128)(2,1)}, bf16[640,768]{1,0:T(8,128)(2,1)}, bf16[640,3072]{1,0:T(8,128)(2,1)}, bf16[640,768]{1,0:T(8,128)(2,1)}, bf16...) custom-call(s32[1]{0:T(128)} %bitcast.flag, ...), custom_call_target="tpu_custom_call", output_to_operand_aliasing={{0}: (9, {}), {1}: (10, {}), {2}: (11, {}), {3}: (12, {})} | custom-call | flops 4529848320 | bytes 15138816 | tf_op jit(solution)/shard_map/text_forward/pallas_call | solution.py:556
  54.5 7.3 %copy.110.image = bf16[16,145,1024]{2,1,0:T(8,128)(2,1)} copy(bf16[16,145,1024]{2,0,1:T(8,128)(2,1)} %param.18) | data formatting | bytes 9502720 | tf_op args[2]
  63.6 2.8 project.3.vals
  67.8 1.8 maximum_select_fusion.weight.wk
  69.6 2.8 project.2.keys
  72.4 11.6 %joining.2 = (bf16[640,768]{1,0:T(8,128)(2,1)}, bf16[640,768]{1,0:T(8,128)(2,1)}, bf16[640,3072]{1,0:T(8,128)(2,1)}, bf16[640,768]{1,0:T(8,128)(2,1)}, f32[640,7...) custom-call(s32[1]{0:T(128)} %bitcast.flag, ...), custom_call_target="tpu_custom_call", output_to_operand_aliasing={{0}: (17, {}), {1}: (18, {}), {2}: (19, {}), {3}: (20, {})} | custom-call | flops 10569646080 | bytes 25853952 | tf_op jit(solution)/shard_map/joining/pallas_call | solution.py:556
  84.0 8.2 %joining.3 = (bf16[640,768]{1,0:T(8,128)(2,1)}, bf16[640,768]{1,0:T(8,128)(2,1)}, bf16[640,3072]{1,0:T(8,128)(2,1)}, bf16[640,768]{1,0:T(8,128)(2,1)}, f32[640,7...) custom-call(s32[1]{0:T(128)} %bitcast.flag, ...), custom_call_target="tpu_custom_call", output_to_operand_aliasing={{0}: (17, {}), {1}: (18, {}), {2}: (19, {}), {3}: (20, {}),... | custom-call | flops 10569646080 | bytes 25853952 | tf_op jit(solution)/shard_map/joining/pallas_call | solution.py:556
  92.3 3.6 weight_grad.10
  97.3 3.7 weight_grad.11
  104.9 5.1 image_back.1
  110.1 2.9 pad_maximum_fusion
  114.7 1.9 copy-done
  116.5 2.3 collective-permute-start.27
  118.8 2.2 copy.113
  122.3 148.9 %collective-permute-done.5.grad = bf16[320,768]{1,0:T(8,128)(2,1)S(1)} collective-permute-done((bf16[320,768]{1,0:T(8,128)(2,1)S(1)}, bf16[320,768]{1,0:T(8,128)(2,1)S(1)}, u32[]{:S(2)}, u32[]{:S(2)}) %collective-permute-start.5) | collective-permute-done | bytes 491552 | tf_op jit(solution)/shard_map/ppermute | solution.py:713
  272.0 10.5 %text_ffn_back.2 = (bf16[640,768]{1,0:T(8,128)(2,1)}, bf16[640,3072]{1,0:T(8,128)(2,1)}, f32[2,3,2,8,768]{4,3,2,1,0:T(8,128)}, f32[320,768]{1,0:T(8,128)}) custom-call(s32[1]{0:T(128)} %bitcast.flag, f32[2,768]{1,0:T(2,128)} %bitcast.233, bf16[320,768]{1,0:T(8,128)(2,1)} %copy-done.8, ...), custom_call_target="tpu_custom_call", output_to_operand_aliasing={{0}: (7, {}), {1}: (8, {}), {2}: (9, {})} | custom-call | flops 3019898880 | bytes 12386304 | tf_op jit(solution)/shard_map/text_ffn_back/pallas_call | solution.py:556
  283.3 10.7 %text_ffn_back.3 = (bf16[640,768]{1,0:T(8,128)(2,1)}, bf16[640,3072]{1,0:T(8,128)(2,1)}, f32[2,3,2,8,768]{4,3,2,1,0:T(8,128)}, f32[320,768]{1,0:T(8,128)}) custom-call(s32[1]{0:T(128)} %bitcast.flag, f32[2,768]{1,0:T(2,128)} %bitcast.234, bf16[320,768]{1,0:T(8,128)(2,1)} %copy-done.7, ...), custom_call_target="tpu_custom_call", output_to_operand_aliasing={{0}: (7, {}), {1}: (8, {}), {2}: (9, {})} | custom-call | flops 3019898880 | bytes 12386304 | tf_op jit(solution)/shard_map/text_ffn_back/pallas_call | solution.py:556
  294.0 15.8 %text_self_back.2 = (bf16[640,768]{1,0:T(8,128)(2,1)}, bf16[640,2304]{1,0:T(8,128)(2,1)}, f32[640,768]{1,0:T(8,128)}, f32[2,3,2,8,768]{4,3,2,1,0:T(8,128)}) custom-call(s32[1]{0:T(128)} %bitcast.flag, f32[2,768]{1,0:T(2,128)} %bitcast.235, ...), custom_call_target="tpu_custom_call", output_to_operand_aliasing={{0}: (8, {}), {1}: (9, {}), {2}: (10, {}), {3}: (11, {})} | custom-call | flops 1509949440 | bytes 7790592 | tf_op jit(solution)/shard_map/text_self_back/pallas_call | solution.py:556
  309.9 15.8 %text_self_back.3 = (bf16[640,768]{1,0:T(8,128)(2,1)}, bf16[640,2304]{1,0:T(8,128)(2,1)}, f32[640,768]{1,0:T(8,128)}, f32[2,3,2,8,768]{4,3,2,1,0:T(8,128)}) custom-call(s32[1]{0:T(128)} %bitcast.flag, f32[2,768]{1,0:T(2,128)} %bitcast.236, ...), custom_call_target="tpu_custom_call", output_to_operand_aliasing={{0}: (8, {}), {1}: (9, {}), {2}: (10, {}), {3}: (11, {})} | custom-call | flops 1509949440 | bytes 7790592 | tf_op jit(solution)/shard_map/text_self_back/pallas_call | solution.py:556
  327.5 3.7 weight_grad.7
  332.8 6.5 %weight_grad.6 = bf16[768,2304]{1,0:T(8,128)(2,1)} custom-call(bf16[640,768]{1,0:T(8,128)(2,1)} %maximum_select_fusion.1.left, bf16[640,2304]{1,0:T(8,128)(2,1)} %get-tuple-element.148.right), custom_call_target="tpu_custom_call" | custom-call | flops 2264924160 | bytes 7471104 | tf_op jit(solution)/shard_map/weight_grad/pallas_call | solution.py:533
  339.3 2.8 dynamic-slice_bitcast_fusion.3
  342.6 7.7 %weight_grad.8 = bf16[768,3072]{1,0:T(8,128)(2,1)} custom-call(bf16[640,768]{1,0:T(8,128)(2,1)} %get-tuple-element.152.left, bf16[640,3072]{1,0:T(8,128)(2,1)} %get-tuple-element.153.right), custom_call_target="tpu_custom_call" | custom-call | flops 3019898880 | bytes 9633792 | tf_op jit(solution)/shard_map/weight_grad/pallas_call | solution.py:533
  352.1 3.2 dynamic-slice_bitcast_fusion.2
  355.3 6.3 %collective-permute-done.13 = bf16[4,64,768]{2,1,0:T(8,128)(2,1)S(1)} collective-permute-done((bf16[4,64,768]{2,1,0:T(8,128)(2,1)S(1)}, bf16[4,64,768]{2,1,0:T(8,128)(2,1)S(1)}, u32[]{:S(2)}, u32[]{:S(2)}) %collective-permute-start.13) | collective-permute-done | bytes 393248 | tf_op jit(solution)/shard_map/ppermute | solution.py:584
  364.0 7.8 %weight_grad.9 = bf16[3072,768]{1,0:T(8,128)(2,1)} custom-call(bf16[640,3072]{1,0:T(8,128)(2,1)} %get-tuple-element.154.left, bf16[640,768]{1,0:T(8,128)(2,1)} %get-tuple-element.155.right), custom_call_target="tpu_custom_call" | custom-call | flops 3019898880 | bytes 9633792 | tf_op jit(solution)/shard_map/weight_grad/pallas_call | solution.py:533
  373.8 3.3 dynamic-slice_bitcast_fusion.1
  377.2 1.7 collective-permute-done.15
  378.9 3.1 collective-permute-done.16
  385.9 1.9 fusion.3
  389.5 3.4 convert_select_fusion
  392.9 4.9 copy.130
  397.9 2.6 fusion
  400.5 2.4 fusion.1
  403.8 2.6 fusion.2
  406.4 4.0 collective-permute-done.8
  413.2 1.9 collective-permute-start.9
  416.9 9.0 %collective-permute-done.10 = bf16[48,2304]{1,0:T(8,128)(2,1)S(1)} collective-permute-done((bf16[48,2304]{1,0:T(8,128)(2,1)S(1)}, bf16[48,2304]{1,0:T(8,128)(2,1)S(1)}, u32[]{:S(2)}, u32[]{:S(2)}) %collective-permute-start.10) | collective-permute-done | bytes 221216 | tf_op jit(solution)/shard_map/ppermute | solution.py:584
  426.7 4.4 collective-permute-done.11
  431.9 3.7 collective-permute-done.23
  437.9 22.7 %collective-permute-done.18 = bf16[4,48,3072]{2,1,0:T(8,128)(2,1)S(1)} collective-permute-done((bf16[4,48,3072]{2,1,0:T(8,128)(2,1)S(1)}, bf16[4,48,3072]{2,1,0:T(8,128)(2,1)S(1)}, u32[]{:S(2)}, u32[]{:S(2)}) %collective-permute-start.18) | collective-permute-done | bytes 1179680 | tf_op jit(solution)/shard_map/ppermute | solution.py:584
  465.1 7.4 %collective-permute-done.19 = bf16[48,3072]{1,0:T(8,128)(2,1)S(1)} collective-permute-done((bf16[48,3072]{1,0:T(8,128)(2,1)S(1)}, bf16[48,3072]{1,0:T(8,128)(2,1)S(1)}, u32[]{:S(2)}, u32[]{:S(2)}) %collective-permute-start.19) | collective-permute-done | bytes 294944 | tf_op jit(solution)/shard_map/ppermute | solution.py:584
  473.2 9.9 %collective-permute-done.20 = bf16[48,3072]{1,0:T(8,128)(2,1)S(1)} collective-permute-done((bf16[48,3072]{1,0:T(8,128)(2,1)S(1)}, bf16[48,3072]{1,0:T(8,128)(2,1)S(1)}, u32[]{:S(2)}, u32[]{:S(2)}) %collective-permute-start.20) | collective-permute-done | bytes 294944 | tf_op jit(solution)/shard_map/ppermute | solution.py:584
  483.7 12.7 %collective-permute-done.21 = bf16[48,3072]{1,0:T(8,128)(2,1)S(1)} collective-permute-done((bf16[48,3072]{1,0:T(8,128)(2,1)S(1)}, bf16[48,3072]{1,0:T(8,128)(2,1)S(1)}, u32[]{:S(2)}, u32[]{:S(2)}) %collective-permute-start.21) | collective-permute-done | bytes 294944 | tf_op jit(solution)/shard_map/ppermute | solution.py:584
  500.0 4.8 collective-permute-done.26
  505.8 21.7 %collective-permute-done.32 = bf16[128,768]{1,0:T(8,128)(2,1)S(1)} collective-permute-done((bf16[128,768]{1,0:T(8,128)(2,1)S(1)}, bf16[128,768]{1,0:T(8,128)(2,1)S(1)}, u32[]{:S(2)}, u32[]{:S(2)}) %collective-permute-start.32) | collective-permute-done | bytes 196640 | tf_op jit(solution)/shard_map/ppermute | solution.py:812
  (153 shorter events, 55.7 us)
Async XLA Ops:
  1.9 61.2 %collective-permute-start.1 = (bf16[512,768]{1,0:T(8,128)(2,1)S(1)}, bf16[512,768]{1,0:T(8,128)(2,1)S(1)}, u32[]{:S(2)}, u32[]{:S(2)}) collective-permute-start(bf16[512,768]{1,0:T(8,128)(2,1)S(1)} %constant_dynamic-slice_fusion), channel_id=1, source_target_pairs={{0,16},{1,17},{2,18},{3,19},{4,20},{5,21},{6,22},{7,23},{8,24},{9,... | collective-permute-start | bytes 2359304 | tf_op jit(solution)/shard_map/ppermute | solution.py:633
  29.3 37.2 %collective-permute-start.3 = (bf16[320,768]{1,0:T(8,128)(2,1)}, bf16[320,768]{1,0:T(8,128)(2,1)S(1)}, u32[]{:S(2)}, u32[]{:S(2)}) collective-permute-start(bf16[320,768]{1,0:T(8,128)(2,1)} %get-tuple-element.93), channel_id=1, source_target_pairs={{0,16},{1,17},{2,18},{3,19},{4,20},{5,21},{6,22},{7,23},{8,24},{9,... | collective-permute-start | bytes 1474568 | tf_op jit(solution)/shard_map/ppermute | solution.py:682
  53.1 13.4 %collective-permute-start = (bf16[320,768]{1,0:T(8,128)(2,1)}, bf16[320,768]{1,0:T(8,128)(2,1)S(1)}, u32[]{:S(2)}, u32[]{:S(2)}) collective-permute-start(bf16[320,768]{1,0:T(8,128)(2,1)} %get-tuple-element.92), channel_id=1, source_target_pairs={{0,16},{1,17},{2,18},{3,19},{4,20},{5,21},{6,22},{7,23},{8,24},{9,... | collective-permute-start | bytes 1474568 | tf_op jit(solution)/shard_map/ppermute | solution.py:682
  54.5 7.3 %copy-start.9 = (f32[768]{0:T(1024)S(1)}, f32[768]{0:T(1024)}, u32[]{:S(2)}) copy-start(f32[768]{0:T(1024)} %param.30) | copy-start | bytes 9220
  54.5 7.9 %copy-start.10 = (f32[768]{0:T(1024)S(1)}, f32[768]{0:T(1024)}, u32[]{:S(2)}) copy-start(f32[768]{0:T(1024)} %param.31) | copy-start | bytes 9220
  54.5 8.5 %copy-start.11 = (s32[4,4]{1,0:T(4,128)S(1)}, s32[4,4]{1,0:T(4,128)}, u32[]{:S(2)}) copy-start(s32[4,4]{1,0:T(4,128)} %param.20) | copy-start | bytes 196
  63.0 4.7 collective-permute-start.2
  66.5 3.1 copy-start.6
  66.5 3.1 copy-start.4
  97.3 5.1 copy-start.12
  102.3 168.9 %collective-permute-start.5 = (bf16[320,768]{1,0:T(8,128)(2,1)S(1)}, bf16[320,768]{1,0:T(8,128)(2,1)S(1)}, u32[]{:S(2)}, u32[]{:S(2)}) collective-permute-start(bf16[320,768]{1,0:T(8,128)(2,1)S(1)} %copy-done.12), channel_id=1, source_target_pairs={{16,0},{17,1},{18,2},{19,3},{20,4},{21,5},{22,6},{23,7},{24,8},{25... | collective-permute-start | bytes 1474568 | tf_op jit(solution)/shard_map/ppermute | solution.py:713
  103.6 178.9 %collective-permute-start.4 = (bf16[320,768]{1,0:T(8,128)(2,1)}, bf16[320,768]{1,0:T(8,128)(2,1)S(1)}, u32[]{:S(2)}, u32[]{:S(2)}) collective-permute-start(bf16[320,768]{1,0:T(8,128)(2,1)} %get-tuple-element.115), channel_id=1, source_target_pairs={{16,0},{17,1},{18,2},{19,3},{20,4},{21,5},{22,6},{23,7},{24,8},{25... | collective-permute-start | bytes 1474568 | tf_op jit(solution)/shard_map/ppermute | solution.py:713
  113.0 3.6 copy-start
  113.0 5.8 %copy-start.3 = (bf16[16,145,512]{2,1,0:T(8,128)(2,1)S(1)}, bf16[16,145,512]{2,1,0:T(8,128)(2,1)}, u32[]{:S(2)}) copy-start(bf16[16,145,512]{2,1,0:T(8,128)(2,1)} %get-tuple-element.146) | copy-start | bytes 7127044
  116.5 281.3 %collective-permute-start.27 = (bf16[8,224,768]{2,1,0:T(8,128)(2,1)}, bf16[8,224,768]{2,1,0:T(8,128)(2,1)}, u32[]{:S(2)}, u32[]{:S(2)}) collective-permute-start(bf16[8,224,768]{2,1,0:T(8,128)(2,1)} %dynamic-slice_bitcast_fusion), channel_id=1, source_target_pairs={{16,17},{17,16},{18,19},{19,18},{20,21},{21,20},{22,23},{23,22},{2... | collective-permute-start | bytes 8257544 | tf_op jit(solution)/shard_map/ppermute | solution.py:584
  121.0 268.4 %collective-permute-start.6 = (bf16[16,145,512]{2,0,1:T(8,128)(2,1)}, bf16[16,145,512]{2,0,1:T(8,128)(2,1)}, u32[]{:S(2)}, u32[]{:S(2)}) collective-permute-start(bf16[16,145,512]{2,0,1:T(8,128)(2,1)} %copy.113), channel_id=1, source_target_pairs={{16,0},{17,1},{18,2},{19,3},{20,4},{21,5},{22,6},{23,7},{24,8},{25... | collective-permute-start | bytes 7127048 | tf_op jit(solution)/shard_map/ppermute | solution.py:746
  332.7 17.5 %collective-permute-start.12 = (bf16[8,64,768]{2,1,0:T(8,128)(2,1)S(1)}, bf16[8,64,768]{2,1,0:T(8,128)(2,1)S(1)}, u32[]{:S(2)}, u32[]{:S(2)}) collective-permute-start(bf16[8,64,768]{2,1,0:T(8,128)(2,1)S(1)} %dynamic-slice_bitcast_fusion.8), channel_id=1, source_target_pairs={{0,1},{1,0},{2,3},{3,2},{4,5},{5,4},{6,7},{7,6},{8,9},{9,8},{10,11... | collective-permute-start | bytes 2359304 | tf_op jit(solution)/shard_map/ppermute | solution.py:584
  342.1 43.8 %collective-permute-start.7 = (bf16[8,48,2304]{2,1,0:T(8,128)(2,1)}, bf16[8,48,2304]{2,1,0:T(8,128)(2,1)}, u32[]{:S(2)}, u32[]{:S(2)}) collective-permute-start(bf16[8,48,2304]{2,1,0:T(8,128)(2,1)} %dynamic-slice_bitcast_fusion.3), channel_id=1, source_target_pairs={{0,1},{1,0},{2,3},{3,2},{4,5},{5,4},{6,7},{7,6},{8,9},{9,8},{10,11... | collective-permute-start | bytes 5308424 | tf_op jit(solution)/shard_map/ppermute | solution.py:584
  350.5 11.1 %collective-permute-start.13 = (bf16[4,64,768]{2,1,0:T(8,128)(2,1)S(1)}, bf16[4,64,768]{2,1,0:T(8,128)(2,1)S(1)}, u32[]{:S(2)}, u32[]{:S(2)}) collective-permute-start(bf16[4,64,768]{2,1,0:T(8,128)(2,1)S(1)} %dynamic-slice_bitcast_fusion.9), channel_id=1, source_target_pairs={{0,2},{1,3},{2,0},{3,1},{4,6},{5,7},{6,4},{7,5},{8,10},{9,11},{10,... | collective-permute-start | bytes 1179656 | tf_op jit(solution)/shard_map/ppermute | solution.py:584
  362.4 9.8 %collective-permute-start.14 = (bf16[64,768]{1,0:T(8,128)(2,1)S(1)}, bf16[64,768]{1,0:T(8,128)(2,1)S(1)}, u32[]{:S(2)}, u32[]{:S(2)}) collective-permute-start(bf16[64,768]{1,0:T(8,128)(2,1)S(1)} %get-tuple-element.236), channel_id=1, source_target_pairs={{0,4},{1,5},{2,6},{3,7},{4,0},{5,1},{6,2},{7,3},{8,12},{9,13},{10,... | collective-permute-start | bytes 294920 | tf_op jit(solution)/shard_map/ppermute | solution.py:584
  371.8 7.0 %collective-permute-start.15 = (bf16[64,768]{1,0:T(8,128)(2,1)}, bf16[64,768]{1,0:T(8,128)(2,1)S(1)}, u32[]{:S(2)}, u32[]{:S(2)}) collective-permute-start(bf16[64,768]{1,0:T(8,128)(2,1)} %get-tuple-element.238), channel_id=1, source_target_pairs={{0,8},{1,9},{2,10},{3,11},{4,12},{5,13},{6,14},{7,15},{8,0},{9,1},... | collective-permute-start | bytes 294920 | tf_op jit(solution)/shard_map/ppermute | solution.py:584
  372.3 9.7 %collective-permute-start.16 = (bf16[64,768]{1,0:T(8,128)(2,1)}, bf16[64,768]{1,0:T(8,128)(2,1)S(1)}, u32[]{:S(2)}, u32[]{:S(2)}) collective-permute-start(bf16[64,768]{1,0:T(8,128)(2,1)} %get-tuple-element.237), channel_id=1, source_target_pairs={{0,12},{1,13},{2,14},{3,15},{4,8},{5,9},{6,10},{7,11},{8,4},{9,5},... | collective-permute-start | bytes 294920 | tf_op jit(solution)/shard_map/ppermute | solution.py:584
  373.8 12.1 %copy-start.2 = (bf16[768,2304]{1,0:T(8,128)(2,1)S(1)}, bf16[768,2304]{1,0:T(8,128)(2,1)}, u32[]{:S(2)}) copy-start(bf16[768,2304]{1,0:T(8,128)(2,1)} %weight_grad.6) | copy-start | bytes 10616836
  378.9 21.6 %collective-permute-start.22 = (bf16[8,192,768]{2,1,0:T(8,128)(2,1)}, bf16[8,192,768]{2,1,0:T(8,128)(2,1)}, u32[]{:S(2)}, u32[]{:S(2)}) collective-permute-start(bf16[8,192,768]{2,1,0:T(8,128)(2,1)} %dynamic-slice_bitcast_fusion.1), channel_id=1, source_target_pairs={{0,1},{1,0},{2,3},{3,2},{4,5},{5,4},{6,7},{7,6},{8,9},{9,8},{10,11... | collective-permute-start | bytes 7077896 | tf_op jit(solution)/shard_map/ppermute | solution.py:584
  381.9 21.9 %collective-permute-start.17 = (bf16[8,48,3072]{2,1,0:T(8,128)(2,1)}, bf16[8,48,3072]{2,1,0:T(8,128)(2,1)}, u32[]{:S(2)}, u32[]{:S(2)}) collective-permute-start(bf16[8,48,3072]{2,1,0:T(8,128)(2,1)} %dynamic-slice_bitcast_fusion.2), channel_id=1, source_target_pairs={{0,1},{1,0},{2,3},{3,2},{4,5},{5,4},{6,7},{7,6},{8,9},{9,8},{10,11... | collective-permute-start | bytes 7077896 | tf_op jit(solution)/shard_map/ppermute | solution.py:584
  387.8 10.1 %slice-start = ((s8[5505024]{0:T(1024)(128)(4,1)}), s8[4194304]{0:T(1024)(128)(4,1)S(1)}, s32[]{:S(2)}) async-start(s8[5505024]{0:T(1024)(128)(4,1)} %bitcast.192), calls=%async_computation | async-start | bytes 8388608
  387.9 22.5 %collective-permute-start.8 = (bf16[4,48,2304]{2,1,0:T(8,128)(2,1)S(1)}, bf16[4,48,2304]{2,1,0:T(8,128)(2,1)S(1)}, u32[]{:S(2)}, u32[]{:S(2)}) collective-permute-start(bf16[4,48,2304]{2,1,0:T(8,128)(2,1)S(1)} %dynamic-slice_bitcast_fusion.7), channel_id=1, source_target_pairs={{0,2},{1,3},{2,0},{3,1},{4,6},{5,7},{6,4},{7,5},{8,10},{9,11},{10,... | collective-permute-start | bytes 2654216 | tf_op jit(solution)/shard_map/ppermute | solution.py:584
  389.5 8.4 %slice-start.1 = ((s8[5505024]{0:T(1024)(128)(4,1)}), s8[1310720]{0:T(1024)(128)(4,1)S(1)}, s32[]{:S(2)}) async-start(s8[5505024]{0:T(1024)(128)(4,1)} %bitcast.192), calls=%async_computation.1 | async-start | bytes 2621440
  389.5 11.0 %slice-start.4 = ((s8[4718592]{0:T(1024)(128)(4,1)}), s8[4194304]{0:T(1024)(128)(4,1)S(1)}, s32[]{:S(2)}) async-start(s8[4718592]{0:T(1024)(128)(4,1)} %bitcast.214), calls=%async_computation.4 | async-start | bytes 8388608
  392.9 7.6 %slice-start.5 = ((s8[4718592]{0:T(1024)(128)(4,1)}), s8[524288]{0:T(1024)(128)(4,1)S(1)}, s32[]{:S(2)}) async-start(s8[4718592]{0:T(1024)(128)(4,1)} %bitcast.214), calls=%async_computation.5 | async-start | bytes 1048576
  397.8 5.9 %slice-start.2 = ((s8[4718592]{0:T(1024)(128)(4,1)}), s8[524288]{0:T(1024)(128)(4,1)S(1)}, s32[]{:S(2)}) async-start(s8[4718592]{0:T(1024)(128)(4,1)} %bitcast.210), calls=%async_computation.2 | async-start | bytes 1048576
  400.4 3.3 slice-start.3
  403.0 32.6 %collective-permute-start.23 = (bf16[4,192,768]{2,1,0:T(8,128)(2,1)S(1)}, bf16[4,192,768]{2,1,0:T(8,128)(2,1)S(1)}, u32[]{:S(2)}, u32[]{:S(2)}) collective-permute-start(bf16[4,192,768]{2,1,0:T(8,128)(2,1)S(1)} %dynamic-slice_bitcast_fusion.5), channel_id=1, source_target_pairs={{0,2},{1,3},{2,0},{3,1},{4,6},{5,7},{6,4},{7,5},{8,10},{9,11},{10,... | collective-permute-start | bytes 3538952 | tf_op jit(solution)/shard_map/ppermute | solution.py:584
  410.7 15.3 %collective-permute-start.10 = (bf16[48,2304]{1,0:T(8,128)(2,1)S(1)}, bf16[48,2304]{1,0:T(8,128)(2,1)S(1)}, u32[]{:S(2)}, u32[]{:S(2)}) collective-permute-start(bf16[48,2304]{1,0:T(8,128)(2,1)S(1)} %get-tuple-element.233), channel_id=1, source_target_pairs={{0,8},{1,9},{2,10},{3,11},{4,12},{5,13},{6,14},{7,15},{8,0},{9,1},... | collective-permute-start | bytes 663560 | tf_op jit(solution)/shard_map/ppermute | solution.py:584
  411.5 19.5 %collective-permute-start.11 = (bf16[48,2304]{1,0:T(8,128)(2,1)S(1)}, bf16[48,2304]{1,0:T(8,128)(2,1)S(1)}, u32[]{:S(2)}, u32[]{:S(2)}) collective-permute-start(bf16[48,2304]{1,0:T(8,128)(2,1)S(1)} %get-tuple-element.232), channel_id=1, source_target_pairs={{0,12},{1,13},{2,14},{3,15},{4,8},{5,9},{6,10},{7,11},{8,4},{9,5},... | collective-permute-start | bytes 663560 | tf_op jit(solution)/shard_map/ppermute | solution.py:584
  413.2 17.9 %collective-permute-start.9 = (bf16[48,2304]{1,0:T(8,128)(2,1)S(1)}, bf16[48,2304]{1,0:T(8,128)(2,1)S(1)}, u32[]{:S(2)}, u32[]{:S(2)}) collective-permute-start(bf16[48,2304]{1,0:T(8,128)(2,1)S(1)} %get-tuple-element.231), channel_id=1, source_target_pairs={{0,4},{1,5},{2,6},{3,7},{4,0},{5,1},{6,2},{7,3},{8,12},{9,13},{10,... | collective-permute-start | bytes 663560 | tf_op jit(solution)/shard_map/ppermute | solution.py:584
  415.2 45.4 %collective-permute-start.18 = (bf16[4,48,3072]{2,1,0:T(8,128)(2,1)S(1)}, bf16[4,48,3072]{2,1,0:T(8,128)(2,1)S(1)}, u32[]{:S(2)}, u32[]{:S(2)}) collective-permute-start(bf16[4,48,3072]{2,1,0:T(8,128)(2,1)S(1)} %dynamic-slice_bitcast_fusion.6), channel_id=1, source_target_pairs={{0,2},{1,3},{2,0},{3,1},{4,6},{5,7},{6,4},{7,5},{8,10},{9,11},{10,... | collective-permute-start | bytes 3538952 | tf_op jit(solution)/shard_map/ppermute | solution.py:584
  425.9 37.0 %collective-permute-start.28 = (bf16[4,224,768]{2,1,0:T(8,128)(2,1)S(1)}, bf16[4,224,768]{2,1,0:T(8,128)(2,1)S(1)}, u32[]{:S(2)}, u32[]{:S(2)}) collective-permute-start(bf16[4,224,768]{2,1,0:T(8,128)(2,1)S(1)} %dynamic-slice_bitcast_fusion.4), channel_id=1, source_target_pairs={{16,18},{17,19},{18,16},{19,17},{20,22},{21,23},{22,20},{23,21},{2... | collective-permute-start | bytes 4128776 | tf_op jit(solution)/shard_map/ppermute | solution.py:584
  436.0 63.9 %collective-permute-start.24 = (bf16[192,768]{1,0:T(8,128)(2,1)S(1)}, bf16[192,768]{1,0:T(8,128)(2,1)S(1)}, u32[]{:S(2)}, u32[]{:S(2)}) collective-permute-start(bf16[192,768]{1,0:T(8,128)(2,1)S(1)} %get-tuple-element.223), channel_id=1, source_target_pairs={{0,4},{1,5},{2,6},{3,7},{4,0},{5,1},{6,2},{7,3},{8,12},{9,13},{10,... | collective-permute-start | bytes 884744 | tf_op jit(solution)/shard_map/ppermute | solution.py:584
  437.1 62.9 %collective-permute-start.25 = (bf16[192,768]{1,0:T(8,128)(2,1)S(1)}, bf16[192,768]{1,0:T(8,128)(2,1)S(1)}, u32[]{:S(2)}, u32[]{:S(2)}) collective-permute-start(bf16[192,768]{1,0:T(8,128)(2,1)S(1)} %get-tuple-element.225), channel_id=1, source_target_pairs={{0,8},{1,9},{2,10},{3,11},{4,12},{5,13},{6,14},{7,15},{8,0},{9,1},... | collective-permute-start | bytes 884744 | tf_op jit(solution)/shard_map/ppermute | solution.py:584
  461.1 11.4 %collective-permute-start.19 = (bf16[48,3072]{1,0:T(8,128)(2,1)S(1)}, bf16[48,3072]{1,0:T(8,128)(2,1)S(1)}, u32[]{:S(2)}, u32[]{:S(2)}) collective-permute-start(bf16[48,3072]{1,0:T(8,128)(2,1)S(1)} %get-tuple-element.226), channel_id=1, source_target_pairs={{0,4},{1,5},{2,6},{3,7},{4,0},{5,1},{6,2},{7,3},{8,12},{9,13},{10,... | collective-permute-start | bytes 884744 | tf_op jit(solution)/shard_map/ppermute | solution.py:584
  461.6 21.5 %collective-permute-start.20 = (bf16[48,3072]{1,0:T(8,128)(2,1)S(1)}, bf16[48,3072]{1,0:T(8,128)(2,1)S(1)}, u32[]{:S(2)}, u32[]{:S(2)}) collective-permute-start(bf16[48,3072]{1,0:T(8,128)(2,1)S(1)} %get-tuple-element.228), channel_id=1, source_target_pairs={{0,8},{1,9},{2,10},{3,11},{4,12},{5,13},{6,14},{7,15},{8,0},{9,1},... | collective-permute-start | bytes 884744 | tf_op jit(solution)/shard_map/ppermute | solution.py:584
  462.9 33.5 %collective-permute-start.21 = (bf16[48,3072]{1,0:T(8,128)(2,1)S(1)}, bf16[48,3072]{1,0:T(8,128)(2,1)S(1)}, u32[]{:S(2)}, u32[]{:S(2)}) collective-permute-start(bf16[48,3072]{1,0:T(8,128)(2,1)S(1)} %get-tuple-element.227), channel_id=1, source_target_pairs={{0,12},{1,13},{2,14},{3,15},{4,8},{5,9},{6,10},{7,11},{8,4},{9,5},... | collective-permute-start | bytes 884744 | tf_op jit(solution)/shard_map/ppermute | solution.py:584
  472.5 25.6 %collective-permute-start.29 = (bf16[224,768]{1,0:T(8,128)(2,1)S(1)}, bf16[224,768]{1,0:T(8,128)(2,1)S(1)}, u32[]{:S(2)}, u32[]{:S(2)}) collective-permute-start(bf16[224,768]{1,0:T(8,128)(2,1)S(1)} %get-tuple-element.220), channel_id=1, source_target_pairs={{16,20},{17,21},{18,22},{19,23},{20,16},{21,17},{22,18},{23,19},{2... | collective-permute-start | bytes 1032200 | tf_op jit(solution)/shard_map/ppermute | solution.py:584
  483.1 15.4 %collective-permute-start.30 = (bf16[224,768]{1,0:T(8,128)(2,1)S(1)}, bf16[224,768]{1,0:T(8,128)(2,1)S(1)}, u32[]{:S(2)}, u32[]{:S(2)}) collective-permute-start(bf16[224,768]{1,0:T(8,128)(2,1)S(1)} %get-tuple-element.222), channel_id=1, source_target_pairs={{16,24},{17,25},{18,26},{19,27},{20,28},{21,29},{22,30},{23,31},{2... | collective-permute-start | bytes 1032200 | tf_op jit(solution)/shard_map/ppermute | solution.py:584
  496.4 2.0 collective-permute-start.31
  498.1 6.7 %collective-permute-start.26 = (bf16[192,768]{1,0:T(8,128)(2,1)S(1)}, bf16[192,768]{1,0:T(8,128)(2,1)S(1)}, u32[]{:S(2)}, u32[]{:S(2)}) collective-permute-start(bf16[192,768]{1,0:T(8,128)(2,1)S(1)} %get-tuple-element.224), channel_id=1, source_target_pairs={{0,12},{1,13},{2,14},{3,15},{4,8},{5,9},{6,10},{7,11},{8,4},{9,5},... | collective-permute-start | bytes 884744 | tf_op jit(solution)/shard_map/ppermute | solution.py:584
  498.7 28.9 %collective-permute-start.32 = (bf16[128,768]{1,0:T(8,128)(2,1)S(1)}, bf16[128,768]{1,0:T(8,128)(2,1)S(1)}, u32[]{:S(2)}, u32[]{:S(2)}) collective-permute-start(bf16[128,768]{1,0:T(8,128)(2,1)S(1)} %fusion.22), channel_id=1, source_target_pairs={{16,0},{17,1},{18,2},{19,3},{20,4},{21,5},{22,6},{23,7},{24,8},{25... | collective-permute-start | bytes 589832 | tf_op jit(solution)/shard_map/ppermute | solution.py:812
  (4 other events, 5.1 us)

commit v2 on v1

--- a/solution.py
+++ b/solution.py
@@ -53,9 +53,8 @@
 
 
 def by_rows(count, body):
-    @pl.loop(0, count // CHUNK)
-    def _(step):
-        body(pl.ds(pl.multiple_of(step * CHUNK, CHUNK), CHUNK))
+    for at in range(0, count, CHUNK):
+        body(pl.ds(at, CHUNK))
 
 
 def standard(summed):
@@ -98,6 +97,20 @@
     return first, 1.0 - first
 
 
+def lanes(value, low, high):
+    return jnp.concatenate([value * low, value * high], 0)
+
+
+def weights_of(scores):
+    grown = [jnp.exp(s - jnp.max(s, 0, keepdims=True)) for s in scores]
+    return [(e * (1.0 / jnp.sum(e, 0, keepdims=True))).astype(BF) for e in grown]
+
+
+def scores_back(weights_b, grad_w):
+    weights = [w.astype(F32) for w in weights_b]
+    return [(w * (g - jnp.sum(g * w, 0, keepdims=True))).astype(BF) for w, g in zip(weights, grad_w)]
+
+
 def self_attend(qkv, mask, probs, att, groups, first_group, span, head_dim):
     width = 2 * head_dim
     model = att.shape[1]
@@ -105,24 +118,19 @@
     low, high = head_lanes(width, head_dim)
     scale = 1.0 / math.sqrt(head_dim)
     low_b, high_b = (low * scale).astype(BF), (high * scale).astype(BF)
+    at = [p * width for p in range(pairs)]
 
     @pl.loop(0, groups)
     def _(g):
         rows = pl.ds(pl.multiple_of(g * span, span), span)
         bias = mask[first_group + g]
-        bias = jnp.concatenate([bias, bias], 0)
-        for p in range(pairs):
-            cols = p * width
-            q = qkv[rows, cols : cols + width]
-            k = qkv[rows, model + cols : model + cols + width]
-            v = qkv[rows, 2 * model + cols : 2 * model + cols + width]
-            both = jnp.concatenate([q * low_b, q * high_b], 0)
-            scores = nt(both, k) + bias
-            grown = jnp.exp(scores - jnp.max(scores, -1, keepdims=True))
-            weights = (grown / jnp.sum(grown, -1, keepdims=True)).astype(BF)
-            probs[g * pairs + p] = weights
-            out = nn(weights, v)
-            att[rows, cols : cols + width] = (out[:span] * low + out[span:] * high).astype(BF)
+        both = [lanes(qkv[rows, c : c + width], low_b, high_b) for c in at]
+        scores = [nt(qkv[rows, model + c : model + c + width], b) + bias for c, b in zip(at, both)]
+        weights = weights_of(scores)
+        for p, c in enumerate(at):
+            probs[g * pairs + p] = weights[p]
+            out = tn(weights[p], qkv[rows, 2 * model + c : 2 * model + c + width])
+            att[rows, c : c + width] = (out[:span] * low + out[span:] * high).astype(BF)
 
 
 def self_attend_back(qkv, probs, grad_att, grad_qkv, groups, span, head_dim):
@@ -131,30 +139,23 @@
     pairs = model // width
     low, high = head_lanes(width, head_dim)
     scale = 1.0 / math.sqrt(head_dim)
-    scaled = ((low * scale).astype(BF), (high * scale).astype(BF))
-    plain = (low.astype(BF), high.astype(BF))
+    low_s, high_s = low * scale, high * scale
+    scaled, plain = (low_s.astype(BF), high_s.astype(BF)), (low.astype(BF), high.astype(BF))
+    at = [p * width for p in range(pairs)]
 
     @pl.loop(0, groups)
     def _(g):
         rows = pl.ds(pl.multiple_of(g * span, span), span)
-        for p in range(pairs):
-            cols = p * width
-            q = qkv[rows, cols : cols + width]
-            k = qkv[rows, model + cols : model + cols + width]
-            v = qkv[rows, 2 * model + cols : 2 * model + cols + width]
-            go = grad_att[rows, cols : cols + width]
-            both_q = jnp.concatenate([q * scaled[0], q * scaled[1]], 0)
-            both_g = jnp.concatenate([go * plain[0], go * plain[1]], 0)
-            weights_b = probs[g * pairs + p]
-            weights = weights_b.astype(F32)
-            grad_w = nt(both_g, v)
-            grad_s = (weights * (grad_w - jnp.sum(grad_w * weights, -1, keepdims=True))).astype(BF)
-            out = nn(grad_s, k)
-            grad_qkv[rows, cols : cols + width] = (
-                out[:span] * (low * scale) + out[span:] * (high * scale)
-            ).astype(BF)
-            grad_qkv[rows, model + cols : model + cols + width] = tn(grad_s, both_q).astype(BF)
-            grad_qkv[rows, 2 * model + cols : 2 * model + cols + width] = tn(weights_b, both_g).astype(BF)
+        both_g = [lanes(grad_att[rows, c : c + width], *plain) for c in at]
+        weights = [probs[g * pairs + p] for p in range(pairs)]
+        grad_w = [nt(qkv[rows, 2 * model + c : 2 * model + c + width], b) for c, b in zip(at, both_g)]
+        grad_s = scores_back(weights, grad_w)
+        for p, c in enumerate(at):
+            out = tn(grad_s[p], qkv[rows, model + c : model + c + width])
+            both_q = lanes(qkv[rows, c : c + width], *scaled)
+            grad_qkv[rows, c : c + width] = (out[:span] * low_s + out[span:] * high_s).astype(BF)
+            grad_qkv[rows, model + c : model + c + width] = nn(grad_s[p], both_q).astype(BF)
+            grad_qkv[rows, 2 * model + c : 2 * model + c + width] = nn(weights[p], both_g[p]).astype(BF)
 
 
 def cross_attend(queries, keys, vals, image, first_row, probs, out, row_count, length, patches, head_dim):
@@ -163,22 +164,20 @@
     low, high = head_lanes(width, head_dim)
     scale = 1.0 / math.sqrt(head_dim)
     low_s, high_s = low * scale, high * scale
-    shown = lax.broadcasted_iota(jnp.int32, (2 * length, keys.shape[1]), 1) < patches
+    shown = lax.broadcasted_iota(jnp.int32, (keys.shape[1], 2 * length), 0) < patches
+    at = [slice(p * width, p * width + width) for p in range(pairs)]
 
     @pl.loop(0, row_count)
     def _(r):
         rows = pl.ds(pl.multiple_of(r * length, 8), length)
         picked = image[first_row + r]
-        for p in range(pairs):
-            cols = slice(p * width, p * width + width)
-            q = queries[rows, cols]
-            both = jnp.concatenate([q * low_s, q * high_s], 0).astype(BF)
-            scores = jnp.where(shown, nt(both, keys[picked, :, cols]), MASKED)
-            grown = jnp.exp(scores - jnp.max(scores, -1, keepdims=True))
-            weights = (grown / jnp.sum(grown, -1, keepdims=True)).astype(BF)
-            probs[r * pairs + p] = weights
-            got = nn(weights, vals[picked, :, cols])
-            out[rows, cols] = got[:length] * low + got[length:] * high
+        both = [lanes(queries[rows, c], low_s, high_s).astype(BF) for c in at]
+        scores = [jnp.where(shown, nt(keys[picked, :, c], b), MASKED) for c, b in zip(at, both)]
+        weights = weights_of(scores)
+        for p, c in enumerate(at):
+            probs[r * pairs + p] = weights[p]
+            got = tn(weights[p], vals[picked, :, c])
+            out[rows, c] = got[:length] * low + got[length:] * high
 
 
 def cross_attend_back(
@@ -189,25 +188,22 @@
     low, high = head_lanes(width, head_dim)
     scale = 1.0 / math.sqrt(head_dim)
     low_s, high_s = low * scale, high * scale
+    at = [slice(p * width, p * width + width) for p in range(pairs)]
 
     @pl.loop(0, row_count)
     def _(r):
         rows = pl.ds(pl.multiple_of(r * length, 8), length)
         picked = image[first_row + r]
-        for p in range(pairs):
-            cols = slice(p * width, p * width + width)
-            q = queries[rows, cols]
-            go = grad_att[rows, cols]
-            both_q = jnp.concatenate([q * low_s, q * high_s], 0).astype(BF)
-            both_g = jnp.concatenate([go * low, go * high], 0).astype(BF)
-            weights_b = probs[r * pairs + p]
-            weights = weights_b.astype(F32)
-            grad_w = nt(both_g, vals[picked, :, cols])
-            grad_s = (weights * (grad_w - jnp.sum(grad_w * weights, -1, keepdims=True))).astype(BF)
-            got = nn(grad_s, keys[picked, :, cols])
-            grad_q[rows, cols] = got[:length] * low_s + got[length:] * high_s
-            grad_k[picked, :, cols] = tn(grad_s, both_q).astype(BF)
-            grad_v[picked, :, cols] = tn(weights_b, both_g).astype(BF)
+        both_g = [lanes(grad_att[rows, c], low, high).astype(BF) for c in at]
+        weights = [probs[r * pairs + p] for p in range(pairs)]
+        grad_w = [nt(vals[picked, :, c], b) for c, b in zip(at, both_g)]
+        grad_s = scores_back(weights, grad_w)
+        for p, c in enumerate(at):
+            both_q = lanes(queries[rows, c], low_s, high_s).astype(BF)
+            got = tn(grad_s[p], keys[picked, :, c])
+            grad_q[rows, c] = got[:length] * low_s + got[length:] * high_s
+            grad_k[picked, :, c] = nn(grad_s[p], both_q).astype(BF)
+            grad_v[picked, :, c] = nn(weights[p], both_g[p]).astype(BF)
 
 
 def grow(entry, w_up, preact, hidden, slope):
@@ -544,6 +540,220 @@
     )(left, right)
 
 
+TILE = 256
+DEEP = 192
+
+
+class Job:
+    def __init__(self, fill, rows, cols, outs):
+        self.fill, self.rows, self.cols, self.outs = fill, rows, cols, outs
+        self.depth = rows * (cols // TILE)
+
+
+def reduce_kernel(model, *refs):
+    (hidden, df, zb, du, att, da, entry, dqkv, dq, midb, dca, catt, gwk, gwv, small), refs = refs[:15], refs[15:]
+    (down, up, qkv, out, norms, wide_k, wide_v, cross_q, cross_o), refs = refs[:9], refs[9:]
+    (hidden_s, df_s, zb_s, du_s, att_s, da_s, entry_s, dqkv_s, dq_s, midb_s, dca_s, catt_s, gwk_s, gwv_s, small_s,
+     tile, core_in, y_in, z_in, final, load_sems, store_sems, send_sems, recv_sems) = refs
+    section, place = lax.axis_index("section"), lax.axis_index("dp")
+    core, y, z = place % 2, place // 2 % 2, place // 4
+    beside = place + 1 - 2 * core
+    across = place + 2 - 4 * y
+    along = [place + 4 * (1 - 2 * (z % 2)), place + 4 * (2 - 4 * (z // 2)), place + 4 * (3 - 2 * z)]
+    far = [z + 1 - 2 * (z % 2), z + 2 - 4 * (z // 2), 3 - z]
+    barrier = pltpu.get_barrier_semaphore()
+    for other in [beside, across] + along:
+        pl.semaphore_signal(barrier, inc=1, device_id=(section, other), device_id_type=pl.DeviceIdType.MESH)
+
+    def send(number, kind, source, target, other):
+        copy = pltpu.make_async_remote_copy(
+            src_ref=source, dst_ref=target, send_sem=send_sems.at[number, kind], recv_sem=recv_sems.at[number, kind],
+            device_id=(section, other), device_id_type=pl.DeviceIdType.MESH,
+        )
+        copy.start()
+        return copy
+
+    def loads(pairs, first):
+        waits = {}
+        for i, (source, target) in enumerate(pairs):
+            copy = pltpu.make_async_copy(source, target, load_sems.at[first + i])
+            copy.start()
+            waits[id(target)] = copy
+        return waits
+
+    def product(left, right, cols, rows, spare=None):
+        def fill(slot, need):
+            need(left)
+            need(right)
+            got = tn(left[...], right[:, cols]).astype(BF)
+            count = (cols.stop - cols.start) // TILE
+            each = rows + (0 if spare is None else spare.shape[1])
+            for k in range(count):
+                piece = got[:, k * TILE : k * TILE + TILE].reshape(4, 2, 2, rows, TILE)
+                tile[slot, :, :, :, k * each : k * each + rows, :] = piece
+            if spare is not None:
+                need(spare)
+                for k in range(count):
+                    extra = spare[:, :, k * TILE : k * TILE + TILE].reshape(4, 2, 2, each - rows, TILE)
+                    tile[slot, :, :, :, k * each + rows : k * each + each, :] = extra
+
+        return fill
+
+    def shuffled(left, right, rows):
+        def fill(slot, need):
+            need(left)
+            need(right)
+            size = left.shape[1]
+            old = lax.broadcasted_iota(jnp.int32, (size, size), 0)
+            new = lax.broadcasted_iota(jnp.int32, (size, size), 1)
+            own = rows // 2
+            source = new % rows // own * (size // 2) + new // rows * own + new % own
+            order = jnp.where(old == source, 1.0, 0.0).astype(BF)
+            got = tn(nn(left[...], order).astype(BF), right[...]).astype(BF)
+            for k in range(size // TILE):
+                piece = got[:, k * TILE : k * TILE + TILE].reshape(4, 2, 2, rows, TILE)
+                tile[slot, :, :, :, k * rows : k * rows + rows, :] = piece
+
+        return fill
+
+    def copied(source, rows):
+        def fill(slot, need):
+            need(source)
+            for k in range(source.shape[1] // TILE):
+                piece = source[:, k * TILE : k * TILE + TILE].reshape(4, 2, 2, rows, TILE)
+                tile[slot, :, :, :, k * rows : k * rows + rows, :] = piece
+
+        return fill
+
+    def run(jobs, waits):
+        waited = set()
+
+        def need(ref):
+            if id(ref) not in waited:
+                waited.add(id(ref))
+                waits[id(ref)].wait()
+
+        stores, cores, ys, zs = [], {}, {}, {}
+        total = len(jobs)
+        for i in range(total + 4):
+            if i < total:
+                if i >= 3:
+                    cores[i - 3].wait_send()
+                slot, deep = i % 3, pl.ds(0, jobs[i].depth)
+                jobs[i].fill(slot, need)
+                if i == 0:
+                    pl.semaphore_wait(barrier, 5)
+                cores[i] = send(i, 0, tile.at[slot, :, :, 1 - core, deep], core_in.at[i, :, :, deep], beside)
+            j = i - 1
+            if 0 <= j < total:
+                cores[j].wait_recv()
+                deep = pl.ds(0, jobs[j].depth)
+
+                @pl.loop(0, 4)
+                def _(a):
+                    for b in range(2):
+                        core_in[j, a, b, deep, :] = core_in[j, a, b, deep, :] + tile[j % 3, a, b, core, deep, :]
+
+                ys[j] = send(j, 1, core_in.at[j, :, 1 - y, deep], y_in.at[j, :, deep], across)
+            j = i - 3
+            if 0 <= j < total:
+                ys[j].wait_recv()
+                deep = pl.ds(0, jobs[j].depth)
+
+                @pl.loop(0, 4)
+                def _(a):
+                    y_in[j, a, deep, :] = y_in[j, a, deep, :] + core_in[j, a, y, deep, :]
+
+                for step in range(3):
+                    zs[j, step] = send(
+                        j, 2 + step, y_in.at[j, far[step], deep], z_in.at[j, step, deep], along[step]
+                    )
+            j = i - 4
+            if 0 <= j < total:
+                for step in range(3):
+                    zs[j, step].wait_recv()
+                deep = pl.ds(0, jobs[j].depth)
+                final[j, deep, :] = (
+                    y_in[j, z, deep, :].astype(F32) + z_in[j, 0, deep, :].astype(F32)
+                ) + (z_in[j, 1, deep, :].astype(F32) + z_in[j, 2, deep, :].astype(F32))
+                each = jobs[j].rows
+                for k in range(jobs[j].cols // TILE):
+                    row = k * each
+                    for target, first, rows in jobs[j].outs:
+                        copy = pltpu.make_async_copy(
+                            final.at[j, pl.ds(row, rows)], target.at[:, pl.ds(first + k * TILE, TILE)],
+                            store_sems.at[len(stores)],
+                        )
+                        copy.start()
+                        stores.append(copy)
+                        row += rows
+        for i in range(total):
+            if i >= total - 3:
+                cores[i].wait_send()
+            ys[i].wait_send()
+            for step in range(3):
+                zs[i, step].wait_send()
+        for copy in stores:
+            copy.wait()
+
+    part = model // 16
+    high = hidden.shape[1] // 16
+    shared = [(hidden, hidden_s), (df, df_s), (zb, zb_s), (du, du_s), (att, att_s), (da, da_s), (small, small_s),
+              (entry, entry_s), (dqkv, dqkv_s)]
+    jobs = []
+    for at in range(0, model, TILE):
+        jobs.append(Job(product(hidden_s, df_s, slice(at, at + TILE), high), high, TILE, [(down, at, high)]))
+    wide = DEEP // part * TILE
+    for at in range(0, hidden.shape[1], wide):
+        jobs.append(Job(product(zb_s, du_s, slice(at, at + wide), part), part, wide, [(up, at, part)]))
+    for at in range(0, 3 * model, model):
+        jobs.append(Job(product(entry_s, dqkv_s, slice(at, at + model), part), part, model, [(qkv, at, part)]))
+    tail = Job(product(att_s, da_s, slice(0, model), part, small_s), part + small.shape[1], model,
+               [(out, 0, part), (norms, 0, small.shape[1])])
+    jobs.append(tail)
+    tall = gwk.shape[0] // 16
+    joint = [
+        Job(shuffled(dq_s, midb_s, part), part, model, [(cross_q, 0, part)]),
+        Job(shuffled(dca_s, catt_s, part), part, model, [(cross_o, 0, part)]),
+        Job(copied(gwk_s, tall), tall, model, [(wide_k, 0, tall)]),
+        Job(copied(gwv_s, tall), tall, model, [(wide_v, 0, tall)]),
+    ]
+
+    @pl.when(section == 0)
+    def _():
+        run(jobs, loads(shared, 0))
+
+    @pl.when(section == 1)
+    def _():
+        waits = loads([(dq, dq_s), (midb, midb_s), (dca, dca_s), (catt, catt_s), (gwk, gwk_s), (gwv, gwv_s)] + shared, 0)
+        run(joint + jobs, waits)
+
+
+def reduce_all(acts, small, dp):
+    hidden, df, zb, du, att, da, entry, dqkv, dq, midb, dca, catt, gwk, gwv = acts
+    model, part, tall = df.shape[1], df.shape[1] // dp, gwk.shape[0] // dp
+    high = hidden.shape[1] // dp
+    jobs = 14
+    shapes = [(high, model), (part, hidden.shape[1]), (part, 3 * model), (part, model), (small.shape[1], model),
+              (tall, model), (tall, model), (part, model), (part, model)]
+    vm = pltpu.VMEM
+    return pl.pallas_call(
+        functools.partial(reduce_kernel, model),
+        in_specs=[ANY] * 15,
+        out_specs=[ANY] * 9,
+        out_shape=[jax.ShapeDtypeStruct(shape, F32) for shape in shapes],
+        scratch_shapes=[vm(a.shape, BF) for a in list(acts) + [small]] + [
+            vm((3, 4, 2, 2, DEEP, TILE), BF), vm((jobs, 4, 2, DEEP, TILE), BF), vm((jobs, 4, DEEP, TILE), BF),
+            vm((jobs, 3, DEEP, TILE), BF), vm((jobs, DEEP, TILE), F32),
+            pltpu.SemaphoreType.DMA((15,)), pltpu.SemaphoreType.DMA((48,)),
+            pltpu.SemaphoreType.DMA((jobs, 5)), pltpu.SemaphoreType.DMA((jobs, 5)),
+        ],
+        compiler_params=pltpu.CompilerParams(vmem_limit_bytes=LIMIT, collective_id=1, has_side_effects=True),
+        cost_estimate=pl.CostEstimate(flops=20_000_000_000, bytes_accessed=40_000_000, transcendentals=0),
+        name="reduce_all",
+    )(*acts, small)
+
+
 def stage(kernel, name, smem, vmem, hbm, bufs, fresh, scratch, flops):
     arrays = [b for b in bufs if not isinstance(b, jax.ShapeDtypeStruct)]
     first = len(smem) + len(vmem) + len(hbm)
@@ -567,33 +777,22 @@
     return list(got[: len(bufs)]), list(got[len(bufs) :])
 
 
-def spread(value, axis_size):
-    return value.reshape(axis_size, value.shape[0] // axis_size, value.shape[1])
-
-
-def reduce_parts(value, only):
-    total = lax.axis_size("dp")
-    if total != 16:
-        return lax.psum_scatter(value, "dp", scatter_dimension=0, tiled=True)[0].astype(F32)
-    place = lax.axis_index("dp")
-    core, y, z = place % 2, (place // 2) % 2, place // 4
-    rows, cols = value.shape[1:]
-
-    def swap(sent, flip):
-        perm = [(s * total + i, s * total + (i ^ flip)) for s in only for i in range(total)]
-        return lax.ppermute(sent, ("section", "dp"), perm)
-
-    def pick(array, axis, index):
-        return lax.dynamic_index_in_dim(array, index, axis, keepdims=False)
-
-    value = value.reshape(8, 2, rows, cols)
-    got = swap(pick(value, 1, 1 - core), 1)
-    value = (pick(value, 1, core).astype(F32) + got.astype(F32)).astype(BF)
-    value = value.reshape(4, 2, rows, cols)
-    got = swap(pick(value, 1, 1 - y), 2)
-    value = (pick(value, 1, y).astype(F32) + got.astype(F32)).astype(BF)
-    others = [swap(pick(value, 0, z ^ step), 4 * step) for step in (1, 2, 3)]
-    return pick(value, 0, z).astype(F32) + others[0].astype(F32) + others[1].astype(F32) + others[2].astype(F32)
+def reduce_plain(acts, small, dp):
+    hidden, df, zb, du, att, da, entry, dqkv, dq, midb, dca, catt, gwk, gwv = acts
+    model = df.shape[1]
+
+    def total(value):
+        return lax.psum_scatter(value, "dp", scatter_dimension=0, tiled=True).astype(F32)
+
+    def by_owner(value):
+        own = value.reshape(2, dp, model // (2 * dp), model)
+        return jnp.swapaxes(own, 0, 1).reshape(model, model)
+
+    return (
+        total(weight_grad(hidden, df, True)), total(weight_grad(zb, du, False)), total(weight_grad(entry, dqkv, False)),
+        total(weight_grad(att, da, True)), total(small)[0], total(gwk), total(gwv),
+        total(by_owner(weight_grad(dq, midb, True))), total(by_owner(weight_grad(dca, catt, True))),
+    )
 
 
 def per_device(
@@ -620,7 +819,7 @@
     cgain, cbias = cross_gain.reshape(1, model), cross_bias.reshape(1, model)
 
     marks = (segment_ids + segment_ids.shape[1] * (jnp.arange(row_total, dtype=jnp.int32) % 2)[:, None]).reshape(-1, span)
-    mask = jnp.where(marks[:, :, None] == marks[:, None, :], 0.0, MASKED).astype(F32)
+    mask = jnp.where(marks[:, :, None] == jnp.tile(marks, (1, 2))[:, None, :], 0.0, MASKED).astype(F32)
     in_block = jnp.arange(row_total, dtype=jnp.int32) // block_rows * block_rows % half_rows
     image = row_image.reshape(-1) + in_block
 
@@ -659,7 +858,7 @@
         )(flag, images, weight)
 
     vm = pltpu.VMEM
-    probs_shape = (count // span * pairs, 2 * span, span)
+    probs_shape = (count // span * pairs, span, 2 * span)
     text_scratch = [
         vm((count, model), BF), vm(wqkv.shape, BF), vm(wo.shape, BF), vm(w1.shape, BF), vm(w2.shape, BF),
         vm((count, 3 * model), BF), vm(probs_shape, BF), vm((count, model), BF), vm((count, model), F32),
@@ -689,7 +888,7 @@
         vm(cross_query.shape, BF), vm(cross_out.shape, BF), vm((half_rows, PAD, model), BF),
         vm((half_rows, PAD, model), BF), vm((count, model), BF), vm((count, 3 * model), BF), vm(probs_shape, BF),
         vm((count, model), BF), vm((count, model), F32), vm((count, model), F32), vm((count, model), BF),
-        vm((count, model), F32), vm((half_rows * pairs, 2 * length, PAD), BF), vm((count, model), F32),
+        vm((count, model), F32), vm((half_rows * pairs, PAD, 2 * length), BF), vm((count, model), F32),
         vm((count, model), BF), vm((count, model), F32), vm((count, model), BF), vm((count, model), F32),
         vm((count, hidden_width), BF), vm((count, hidden_width), BF), vm((count, model), F32), vm((count, model), BF),
         vm((count, model), BF), vm((count, model), F32), vm((count, hidden_width), BF), vm((count, model), F32),
@@ -745,20 +944,9 @@
     )(flag, images, dkey, dval, key_w, image_kv)
     image_part = lax.ppermute(other_part, "section", [(1, 0)])
 
-    grad_cq = weight_grad(dq, midb, True)
-    grad_co = weight_grad(dca, catt, True)
     sections = lax.axis_size("section")
     cross_rows = model // (sections * dp)
-
-    def by_owner(value):
-        value = value.reshape(sections, dp, cross_rows, model)
-        return jnp.swapaxes(value, 0, 1).reshape(dp, sections * cross_rows, model)
-
-    joint = jnp.concatenate(
-        [spread(grad_wk, dp), spread(grad_wv, dp), by_owner(grad_cq), by_owner(grad_co)], 1
-    )
-    joint = reduce_parts(joint, (1,))
-    image_rows = width // dp
+    image_rows, out_rows = width // dp, model // dp
 
     dmids = []
     for half in range(HALVES):
@@ -774,8 +962,6 @@
             4 * count * model * hidden_width,
         )
         dmids.append(fresh[0])
-    down = reduce_parts(spread(weight_grad(hidden, df, True), dp), (0, 1))
-    up = reduce_parts(spread(weight_grad(zb, du, False), dp), (0, 1))
     for half in range(HALVES):
         y1, y3, qkv, probs, slope = kept[half]
         (da, dqkv, ig, sums), _ = stage(
@@ -789,7 +975,6 @@
             2 * count * 4 * model * model,
         )
     entry = jnp.where(is_text, text_in, jnp.concatenate(outward, 0))
-    qkv_grad = reduce_parts(spread(weight_grad(entry, dqkv, False), dp), (0, 1))
 
     totals = jnp.sum(sums, (0, 3))
     own_norm = totals[:2].reshape(4, dp, model // dp)
@@ -798,21 +983,19 @@
         [jnp.moveaxis(own_norm, 1, 0).reshape(dp, -1), jnp.moveaxis(own_cross, 2, 0).reshape(dp, -1)], 1
     )
     small = jnp.pad(small[:, None, :], ((0, 0), (0, 15), (0, model - small.shape[1]))).astype(BF)
-    last = reduce_parts(jnp.concatenate([spread(weight_grad(att, da, True), dp), small], 1), (0, 1))
-    out_rows = model // dp
-    out_grad, small = last[:out_rows], last[out_rows]
+    acts = (hidden, df, zb, du, att, da, entry, dqkv, dq, midb, dca, catt, grad_wk, grad_wv)
+    got = reduce_all(acts, small, dp) if dp == 16 else reduce_plain(acts, small, dp)
+    down, up, qkv_grad, out_grad, small, wide_k, wide_v, cross_q, cross_o = got
+    small = small[0]
     norm_part = small[: 4 * out_rows].reshape(2, 2, out_rows)
     cross_part = small[4 * out_rows : 4 * out_rows + 2 * sections * cross_rows].reshape(2, sections, cross_rows)
 
-    at = 2 * image_rows
-    cross_q = joint[at : at + sections * cross_rows]
-    cross_o = joint[at + sections * cross_rows :]
     extra = jnp.pad(cross_part[:, 0].reshape(1, -1), ((0, 15), (0, model - 2 * cross_rows)))
-    parcel = jnp.concatenate([joint[:image_rows], cross_q[:cross_rows], cross_o[:cross_rows], extra], 0).astype(BF)
+    parcel = jnp.concatenate([wide_k, cross_q[:cross_rows], cross_o[:cross_rows], extra], 0).astype(BF)
     parcel = lax.ppermute(parcel, "section", [(1, 0)]).astype(F32)
     at = image_rows + 2 * cross_rows
     pick = functools.partial(jnp.where, is_text)
-    grad_kv = pick(parcel[:image_rows], joint[image_rows : 2 * image_rows])
+    grad_kv = pick(parcel[:image_rows], wide_v)
     grad_cross_q = pick(parcel[image_rows : image_rows + cross_rows], cross_q[cross_rows:]).T
     grad_cross_o = pick(parcel[image_rows + cross_rows : at], cross_o[cross_rows:]).T
     grad_cross_g = pick(parcel[at, :cross_rows], cross_part[0, 1])

time: 540 us -> 348 us (0.64)
  the two profiles are of different devices: /device:TPU:16 before, /device:TPU:0 now
where the time goes in v2:
time: 348 us; the launch traced here: 343 us
  Pallas kernels  228 us (66%)
  waiting for transfers between devices  59.3 us (17%)
  local copies, waits for them, and re-layouts  27.3 us (8%)
  other arithmetic  13.5 us (4%)
  starting transfers between devices  12.9 us (4%)
    pallas_call x1, Pallas kernels, reduce_all(): pl.pallas_call(functools.partial(reduce_kernel, model), in_specs=[ANY] *...  113 us
    pallas_call x8, Pallas kernels, stage(): pl.pallas_call(kernel, in_specs=[SMEM] * len(smem) + [VMEM] * len(vmem) +...  104 us
    ppermute x2, waiting for transfers between devices, per_device(): returned.append(lax.ppermute(fresh[0], 'section', [(1, 0)]))  54.4 us
    unnamed x30, local copies, waits for them, and re-layouts  16.9 us
  transfers between devices with their start and end apart: 8, of which 3 were waited for; matrix products, arithmetic and copies ran while one was open for 7% of the time, Pallas kernels for 64%

profile of v2, /device:TPU:0, one launch (start us, length us, event | category | flops | bytes accessed | tf_op | source)
XLA Modules:
  0.0 342.5 jit_solution(865312242287162976)
XLA Ops:
  0.7 1.2 constant_dynamic-slice_fusion
  1.9 4.9 %collective-permute-start.1 = (bf16[512,768]{1,0:T(8,128)(2,1)S(1)}, bf16[512,768]{1,0:T(8,128)(2,1)S(1)}, u32[]{:S(2)}, u32[]{:S(2)}) collective-permute-start(bf16[512,768]{1,0:T(8,128)(2,1)S(1)} %constant_dynamic-slice_fusion), channel_id=1, source_target_pairs={{0,16},{1,17},{2,18},{3,19},{4,20},{5,21},{6,22},{7,23},{8,24},{9,... | collective-permute-start | bytes 2359304 | tf_op jit(solution)/shard_map/ppermute | solution.py:832
  6.8 0.8 broadcast_add_fusion
  7.7 1.0 compare_select_fusion.mask
  8.7 16.1 %text_forward.2 = (bf16[640,768]{1,0:T(8,128)(2,1)}, bf16[640,768]{1,0:T(8,128)(2,1)}, bf16[640,3072]{1,0:T(8,128)(2,1)}, bf16[640,768]{1,0:T(8,128)(2,1)}, bf16...) custom-call(s32[1]{0:T(128)} %bitcast.flag, ...), custom_call_target="tpu_custom_call" | custom-call | flops 4529848320 | bytes 15138816 | tf_op jit(solution)/shard_map/text_forward/pallas_call | solution.py:766
  24.8 1.3 collective-permute-start.3
  26.2 16.3 %text_forward.3 = (bf16[640,768]{1,0:T(8,128)(2,1)}, bf16[640,768]{1,0:T(8,128)(2,1)}, bf16[640,3072]{1,0:T(8,128)(2,1)}, bf16[640,768]{1,0:T(8,128)(2,1)}, bf16...) custom-call(s32[1]{0:T(128)} %bitcast.flag, ...), custom_call_target="tpu_custom_call", output_to_operand_aliasing={{0}: (9, {}), {1}: (10, {}), {2}: (11, {}), {3}: (12, {})} | custom-call | flops 4529848320 | bytes 15138816 | tf_op jit(solution)/shard_map/text_forward/pallas_call | solution.py:766
  42.5 1.5 collective-permute-start
  44.1 7.3 %copy.90.image = bf16[16,145,1024]{2,1,0:T(8,128)(2,1)} copy(bf16[16,145,1024]{2,0,1:T(8,128)(2,1)} %param.18) | data formatting | bytes 9502720 | tf_op args[2]
  51.9 0.6 reshape.89.cbias
  53.1 2.8 project.3.vals
  56.0 1.2 maximum_select_fusion.1.refs_6_
  57.2 1.8 maximum_select_fusion.weight.wk
  59.1 2.8 project.2.keys
  61.9 4.9 %joining.2 = (bf16[640,768]{1,0:T(8,128)(2,1)}, bf16[640,768]{1,0:T(8,128)(2,1)}, bf16[640,3072]{1,0:T(8,128)(2,1)}, bf16[640,768]{1,0:T(8,128)(2,1)}, f32[640,7...) custom-call(s32[1]{0:T(128)} %bitcast.flag, ...), custom_call_target="tpu_custom_call", output_to_operand_aliasing={{0}: (17, {}), {1}: (18, {}), {2}: (19, {}), {3}: (20, {})} | custom-call | flops 10569646080 | bytes 25853952 | tf_op jit(solution)/shard_map/joining/pallas_call | solution.py:766
  66.7 1.3 collective-permute-start.5
  68.0 13.3 %joining.3 = (bf16[640,768]{1,0:T(8,128)(2,1)}, bf16[640,768]{1,0:T(8,128)(2,1)}, bf16[640,3072]{1,0:T(8,128)(2,1)}, bf16[640,768]{1,0:T(8,128)(2,1)}, f32[640,7...) custom-call(s32[1]{0:T(128)} %bitcast.flag, ...), custom_call_target="tpu_custom_call", output_to_operand_aliasing={{0}: (17, {}), {1}: (18, {}), {2}: (19, {}), {3}: (20, {}),... | custom-call | flops 10569646080 | bytes 25853952 | tf_op jit(solution)/shard_map/joining/pallas_call | solution.py:766
  81.4 1.3 collective-permute-start.4
  82.7 5.2 %image_back.1 = (f32[16,145,512]{2,1,0:T(8,128)}, bf16[16,145,512]{2,1,0:T(8,128)(2,1)}, bf16[1024,768]{1,0:T(8,128)(2,1)}, bf16[1024,768]{1,0:T(8,128)(2,1)}) custom-call(s32[1]{0:T(128)} %bitcast.flag, bf16[16,145,1024]{2,1,0:T(8,128)(2,1)} %copy.90.image, bf16[16,160,768]{2,1,0:T(8,128)(2,1)} %get-tuple-element.153.dkey, ...), custom_call_target="tpu_custom_call" | custom-call | flops 16106127360 | bytes 25000000 | tf_op jit(solution)/shard_map/image_back/pallas_call | solution.py:915
  87.8 2.5 copy.93
  90.3 1.3 collective-permute-start.6
  91.6 26.0 %collective-permute-done.5.grad = bf16[320,768]{1,0:T(8,128)(2,1)S(1)} collective-permute-done((bf16[320,768]{1,0:T(8,128)(2,1)}, bf16[320,768]{1,0:T(8,128)(2,1)S(1)}, u32[]{:S(2)}, u32[]{:S(2)}) %collective-permute-start.5) | collective-permute-done | bytes 491552 | tf_op jit(solution)/shard_map/ppermute | solution.py:912
  117.6 0.8 copy-done.5
  118.4 10.0 %text_ffn_back.2 = (bf16[640,768]{1,0:T(8,128)(2,1)}, bf16[640,3072]{1,0:T(8,128)(2,1)}, f32[2,3,2,8,768]{4,3,2,1,0:T(8,128)}, f32[320,768]{1,0:T(8,128)}) custom-call(s32[1]{0:T(128)} %bitcast.flag, f32[2,768]{1,0:T(2,128)} %bitcast.76, bf16[320,768]{1,0:T(8,128)(2,1)} %copy-done.5, ...), custom_call_target="tpu_custom_call", output_to_operand_aliasing={{0}: (7, {}), {1}: (8, {}), {2}: (9, {})} | custom-call | flops 3019898880 | bytes 12386304 | tf_op jit(solution)/shard_map/text_ffn_back/pallas_call | solution.py:766
  128.4 28.5 %collective-permute-done.4.grad = bf16[320,768]{1,0:T(8,128)(2,1)S(1)} collective-permute-done((bf16[320,768]{1,0:T(8,128)(2,1)}, bf16[320,768]{1,0:T(8,128)(2,1)S(1)}, u32[]{:S(2)}, u32[]{:S(2)}) %collective-permute-start.4) | collective-permute-done | bytes 491552 | tf_op jit(solution)/shard_map/ppermute | solution.py:912
  156.9 0.8 copy-done.6
  157.7 26.3 %text_ffn_back.3 = (bf16[640,768]{1,0:T(8,128)(2,1)}, bf16[640,3072]{1,0:T(8,128)(2,1)}, f32[2,3,2,8,768]{4,3,2,1,0:T(8,128)}, f32[320,768]{1,0:T(8,128)}) custom-call(s32[1]{0:T(128)} %bitcast.flag, f32[2,768]{1,0:T(2,128)} %bitcast.77, bf16[320,768]{1,0:T(8,128)(2,1)} %copy-done.6, ...), custom_call_target="tpu_custom_call", output_to_operand_aliasing={{0}: (7, {}), {1}: (8, {}), {2}: (9, {})} | custom-call | flops 3019898880 | bytes 12386304 | tf_op jit(solution)/shard_map/text_ffn_back/pallas_call | solution.py:766
  183.9 8.5 %text_self_back.2 = (bf16[640,768]{1,0:T(8,128)(2,1)}, bf16[640,2304]{1,0:T(8,128)(2,1)}, f32[640,768]{1,0:T(8,128)}, f32[2,3,2,8,768]{4,3,2,1,0:T(8,128)}) custom-call(s32[1]{0:T(128)} %bitcast.flag, f32[2,768]{1,0:T(2,128)} %bitcast.78, ...), custom_call_target="tpu_custom_call", output_to_operand_aliasing={{0}: (8, {}), {1}: (9, {}), {2}: (10, {}), {3}: (11, {})} | custom-call | flops 1509949440 | bytes 7790592 | tf_op jit(solution)/shard_map/text_self_back/pallas_call | solution.py:766
  192.4 8.5 %text_self_back.3 = (bf16[640,768]{1,0:T(8,128)(2,1)}, bf16[640,2304]{1,0:T(8,128)(2,1)}, f32[640,768]{1,0:T(8,128)}, f32[2,3,2,8,768]{4,3,2,1,0:T(8,128)}) custom-call(s32[1]{0:T(128)} %bitcast.flag, f32[2,768]{1,0:T(2,128)} %bitcast.79, ...), custom_call_target="tpu_custom_call", output_to_operand_aliasing={{0}: (8, {}), {1}: (9, {}), {2}: (10, {}), {3}: (11, {})} | custom-call | flops 1509949440 | bytes 7790592 | tf_op jit(solution)/shard_map/text_self_back/pallas_call | solution.py:766
  200.9 1.0 reduce_sum.9
  202.5 0.8 pad.10.refs_14_
  203.3 113.5 %reduce_all.1 = (f32[192,768]{1,0:T(8,128)}, f32[48,3072]{1,0:T(8,128)}, f32[48,2304]{1,0:T(8,128)}, f32[48,768]{1,0:T(8,128)}, f32[16,768]{1,0:T(8,128)}, /*ind...) custom-call(bf16[640,3072]{1,0:T(8,128)(2,1)} %get-tuple-element.157.refs_0_, ...), custom_call_target="tpu_custom_call" | custom-call | flops 20000000000 | bytes 40000000 | tf_op jit(solution)/shard_map/reduce_all/pallas_call | solution.py:740
  316.8 0.9 convert.36
  317.7 0.9 slice.127
  318.6 0.9 slice.128
  319.5 0.8 slice_reduce_fusion.1
  320.5 1.3 collective-permute-start.7
  321.8 0.7 slice_reduce_fusion
  323.2 4.9 %collective-permute-done.7 = bf16[128,768]{1,0:T(8,128)(2,1)S(1)} collective-permute-done((bf16[128,768]{1,0:T(8,128)(2,1)S(1)}, bf16[128,768]{1,0:T(8,128)(2,1)S(1)}, u32[]{:S(2)}, u32[]{:S(2)}) %collective-permute-start.7) | collective-permute-done | bytes 196640 | tf_op jit(solution)/shard_map/ppermute | solution.py:995
  328.1 0.6 broadcast_select_fusion
  328.7 1.6 fusion.2
  330.3 0.7 slice_select_fusion
  331.0 3.2 convert_select_fusion
  334.3 4.9 %copy.100 = f32[16,145,512]{2,0,1:T(8,128)} copy(f32[16,145,512]{2,1,0:T(8,128)S(1)} %convert_select_fusion) | data formatting | bytes 9502720
  339.2 0.8 copy.146
  340.0 0.7 copy.147
  340.7 0.8 copy.148
  341.5 0.8 copy.149
  (52 shorter events, 2.8 us)
Async XLA Ops:
  1.9 50.8 %collective-permute-start.1 = (bf16[512,768]{1,0:T(8,128)(2,1)S(1)}, bf16[512,768]{1,0:T(8,128)(2,1)S(1)}, u32[]{:S(2)}, u32[]{:S(2)}) collective-permute-start(bf16[512,768]{1,0:T(8,128)(2,1)S(1)} %constant_dynamic-slice_fusion), channel_id=1, source_target_pairs={{0,16},{1,17},{2,18},{3,19},{4,20},{5,21},{6,22},{7,23},{8,24},{9,... | collective-permute-start | bytes 2359304 | tf_op jit(solution)/shard_map/ppermute | solution.py:832
  24.8 31.1 %collective-permute-start.3 = (bf16[320,768]{1,0:T(8,128)(2,1)}, bf16[320,768]{1,0:T(8,128)(2,1)S(1)}, u32[]{:S(2)}, u32[]{:S(2)}) collective-permute-start(bf16[320,768]{1,0:T(8,128)(2,1)} %get-tuple-element.102), channel_id=1, source_target_pairs={{0,16},{1,17},{2,18},{3,19},{4,20},{5,21},{6,22},{7,23},{8,24},{9,... | collective-permute-start | bytes 1474568 | tf_op jit(solution)/shard_map/ppermute | solution.py:881
  42.5 13.5 %collective-permute-start = (bf16[320,768]{1,0:T(8,128)(2,1)}, bf16[320,768]{1,0:T(8,128)(2,1)S(1)}, u32[]{:S(2)}, u32[]{:S(2)}) collective-permute-start(bf16[320,768]{1,0:T(8,128)(2,1)} %get-tuple-element.101), channel_id=1, source_target_pairs={{0,16},{1,17},{2,18},{3,19},{4,20},{5,21},{6,22},{7,23},{8,24},{9,... | collective-permute-start | bytes 1474568 | tf_op jit(solution)/shard_map/ppermute | solution.py:881
  44.0 7.3 %copy-start.9 = (f32[768]{0:T(1024)S(1)}, f32[768]{0:T(1024)}, u32[]{:S(2)}) copy-start(f32[768]{0:T(1024)} %param.30) | copy-start | bytes 9220
  44.0 7.9 %copy-start.10 = (f32[768]{0:T(1024)S(1)}, f32[768]{0:T(1024)}, u32[]{:S(2)}) copy-start(f32[768]{0:T(1024)} %param.31) | copy-start | bytes 9220
  44.1 8.5 %copy-start.11 = (s32[4,4]{1,0:T(4,128)S(1)}, s32[4,4]{1,0:T(4,128)}, u32[]{:S(2)}) copy-start(s32[4,4]{1,0:T(4,128)} %param.20) | copy-start | bytes 196
  52.6 4.6 %collective-permute-start.2 = (bf16[512,768]{1,0:T(8,128)(2,1)S(1)}, bf16[512,768]{1,0:T(8,128)(2,1)S(1)}, u32[]{:S(2)}, u32[]{:S(2)}) collective-permute-start(bf16[512,768]{1,0:T(8,128)(2,1)S(1)} %collective-permute-done.1), channel_id=1, source_target_pairs={{0,1},{1,0},{2,3},{3,2},{4,5},{5,4},{6,7},{7,6},{8,9},{9,8},{10,11... | collective-permute-start | bytes 2359304 | tf_op jit(solution)/shard_map/ppermute | solution.py:833
  53.1 2.8 copy-start
  56.0 3.1 copy-start.4
  56.0 3.1 copy-start.1
  66.7 50.9 %collective-permute-start.5 = (bf16[320,768]{1,0:T(8,128)(2,1)}, bf16[320,768]{1,0:T(8,128)(2,1)S(1)}, u32[]{:S(2)}, u32[]{:S(2)}) collective-permute-start(bf16[320,768]{1,0:T(8,128)(2,1)} %get-tuple-element.127), channel_id=1, source_target_pairs={{16,0},{17,1},{18,2},{19,3},{20,4},{21,5},{22,6},{23,7},{24,8},{25... | collective-permute-start | bytes 1474568 | tf_op jit(solution)/shard_map/ppermute | solution.py:912
  81.4 75.5 %collective-permute-start.4 = (bf16[320,768]{1,0:T(8,128)(2,1)}, bf16[320,768]{1,0:T(8,128)(2,1)S(1)}, u32[]{:S(2)}, u32[]{:S(2)}) collective-permute-start(bf16[320,768]{1,0:T(8,128)(2,1)} %get-tuple-element.124), channel_id=1, source_target_pairs={{16,0},{17,1},{18,2},{19,3},{20,4},{21,5},{22,6},{23,7},{24,8},{25... | collective-permute-start | bytes 1474568 | tf_op jit(solution)/shard_map/ppermute | solution.py:912
  90.3 240.7 %collective-permute-start.6 = (bf16[16,145,512]{2,0,1:T(8,128)(2,1)S(1)}, bf16[16,145,512]{2,0,1:T(8,128)(2,1)}, u32[]{:S(2)}, u32[]{:S(2)}) collective-permute-start(bf16[16,145,512]{2,0,1:T(8,128)(2,1)S(1)} %copy.93), channel_id=1, source_target_pairs={{16,0},{17,1},{18,2},{19,3},{20,4},{21,5},{22,6},{23,7},{24,8},{25... | collective-permute-start | bytes 7127048 | tf_op jit(solution)/shard_map/ppermute | solution.py:945
  117.6 0.8 copy-start.5
  156.9 0.8 copy-start.6
  320.5 7.6 %collective-permute-start.7 = (bf16[128,768]{1,0:T(8,128)(2,1)S(1)}, bf16[128,768]{1,0:T(8,128)(2,1)S(1)}, u32[]{:S(2)}, u32[]{:S(2)}) collective-permute-start(bf16[128,768]{1,0:T(8,128)(2,1)S(1)} %fusion.1), channel_id=1, source_target_pairs={{16,0},{17,1},{18,2},{19,3},{20,4},{21,5},{22,6},{23,7},{24,8},{25... | collective-permute-start | bytes 589832 | tf_op jit(solution)/shard_map/ppermute | solution.py:995
  334.2 5.0 %copy-start.7 = (f32[48,2304]{1,0:T(8,128)S(1)}, f32[48,2304]{1,0:T(8,128)}, u32[]{:S(2)}) copy-start(f32[48,2304]{1,0:T(8,128)} %get-tuple-element.171) | copy-start | bytes 1327108
  334.2 5.7 %copy-start.8 = (f32[48,768]{1,0:T(8,128)S(1)}, f32[48,768]{1,0:T(8,128)}, u32[]{:S(2)}) copy-start(f32[48,768]{1,0:T(8,128)} %get-tuple-element.172) | copy-start | bytes 442372
  334.3 6.4 %copy-start.3 = (f32[48,3072]{1,0:T(8,128)S(1)}, f32[48,3072]{1,0:T(8,128)}, u32[]{:S(2)}) copy-start(f32[48,3072]{1,0:T(8,128)} %get-tuple-element.173) | copy-start | bytes 1769476
  334.3 7.2 %copy-start.2 = (f32[192,768]{1,0:T(8,128)S(1)}, f32[192,768]{1,0:T(8,128)}, u32[]{:S(2)}) copy-start(f32[192,768]{1,0:T(8,128)} %get-tuple-element.174) | copy-start | bytes 1769476
